TPU v7x, 256 devices: a whole 4x4x8 slice. The times are simulated.
256 devices in a mesh: dp: 32 (over y, x, z_hi), expert: 8 (over z_lo, core).
Axes of the slice: x: 4, y: 4, z: 8 (z_hi: 2, z_lo: 4; z = z_hi * 4 + z_lo), core: 2. Of those that a mesh axis runs over, the one named last changes fastest.
Arguments:
- tokens: bfloat16 [32768, 768], P(('dp', 'expert')), may hold values from -6 to 6
- expert_ids: int32 [32768, 1], P(('dp', 'expert')), may hold values from 0 to 7
- gate: float32 [32768], P(('dp', 'expert')), may hold values from 0.2 to 1
- ln_gain: float32 [768], replicated, may hold values from 0.25 to 1.75
- w_in: bfloat16 [8, 768, 3072], P('expert', 'dp'), may hold values from -0.21875 to 0.21875
- w_out: bfloat16 [8, 3072, 768], P('expert', 'dp'), may hold values from -0.109375 to 0.109375
- image_emb: bfloat16 [2048, 768], P(('dp', 'expert')), may hold values from -6 to 6
Outputs:
- token_grad: bfloat16 [32768, 768], P(('dp', 'expert'))
- gate_grad: float32 [32768], P(('dp', 'expert'))
- w_in_grad: float32 [8, 768, 3072], P('expert', 'dp')
- w_out_grad: float32 [8, 3072, 768], P('expert', 'dp')
Inputs may be any that keep to these rules, and one draw needn't show every extreme that they name: `expert_ids`: each token names one expert.
All inputs are finite; a program needn't handle non-finite values.
Results may differ from a plain program's by a relative error of at most 0.028.
Values may be sent and summed in bfloat16 or wider, within the bound.
A program may use at most 64 MiB of HBM per device.

v0:
```python
import jax
import jax.numpy as jnp
from jax import lax
from jax.sharding import PartitionSpec as P

TEXT_LEN = 16


logit_scale = 100.0
norm_eps = 1e-06


def exact_gelu(values):
    return jax.nn.gelu(values, approximate=False)


def layer_norm(inputs, ln_gain):
    average = jnp.mean(inputs, axis=-1, keepdims=True)
    centred = inputs - average
    variance = jnp.mean(centred * centred, axis=-1, keepdims=True)
    inverse = lax.rsqrt(variance + norm_eps)
    scaled = centred * inverse
    return (scaled, inverse, (scaled * ln_gain).astype(jnp.bfloat16))


def unit_rows(values):
    inverse = lax.rsqrt(jnp.sum(values * values, axis=-1, keepdims=True) + norm_eps)
    return (values * inverse, inverse)


def body(tokens, expert_ids, gate, ln_gain, w_in, w_out, image_emb):
    local_experts = w_in.shape[0]
    owners = lax.axis_size("expert")
    experts = local_experts * owners
    token_count = tokens.shape[0]
    width = tokens.shape[1]
    capacity = (5 * token_count + 4 * experts - 1) // (4 * experts)
    inputs = tokens.astype(jnp.float32)
    scaled, inverse, normed = layer_norm(inputs, ln_gain)
    choose = expert_ids[:, 0]
    onehot = (choose[:, None] == jnp.arange(experts, dtype=jnp.int32)[None, :]).astype(jnp.int32)
    before = jnp.cumsum(onehot, axis=0) - onehot
    slot = jnp.sum(before * onehot, axis=1)
    place = jnp.where(slot < capacity, choose * capacity + slot, -1)
    table = (jnp.arange(experts * capacity, dtype=jnp.int32)[:, None] == place[None, :]).astype(
        jnp.bfloat16
    )
    send = jnp.dot(table, normed, preferred_element_type=jnp.float32).astype(jnp.bfloat16)
    received = lax.all_to_all(
        send.reshape(experts, capacity, width), "expert", split_axis=0, concat_axis=1, tiled=True
    )
    full_in, full_out = (
        lax.all_gather(w_in, "dp", axis=1, tiled=True),
        lax.all_gather(w_out, "dp", axis=1, tiled=True),
    )
    pre = jnp.einsum("erd,edh->erh", received, full_in, preferred_element_type=jnp.float32)
    activated, gelu_back = jax.vjp(exact_gelu, pre)
    activated = activated.astype(jnp.bfloat16)
    expert_slots = jnp.einsum(
        "erh,ehd->erd", activated, full_out, preferred_element_type=jnp.float32
    )
    returned = lax.all_to_all(
        expert_slots.astype(jnp.bfloat16), "expert", split_axis=1, concat_axis=0, tiled=True
    )
    expert_out = jnp.einsum(
        "st,sd->td",
        table,
        returned.reshape(experts * capacity, width),
        preferred_element_type=jnp.float32,
    )
    layer_out = inputs + gate[:, None] * expert_out
    pair_count = token_count // TEXT_LEN
    pooled = jnp.mean(layer_out.reshape(pair_count, TEXT_LEN, width), axis=1)
    text_unit, text_inverse = unit_rows(pooled)
    text_emb = text_unit.astype(jnp.bfloat16)
    image_norm = unit_rows(image_emb.astype(jnp.float32))[0].astype(jnp.bfloat16)
    all_images = lax.all_gather(image_norm, ("dp", "expert"), axis=0, tiled=True)
    scores = logit_scale * jnp.einsum(
        "pd,qd->pq", text_emb, all_images, preferred_element_type=jnp.float32
    )
    expscores = jnp.exp(scores)
    row_total = jnp.sum(expscores, axis=1)
    col_total = lax.psum(jnp.sum(expscores, axis=0), ("dp", "expert"))
    block = lax.axis_index("dp") * lax.axis_size("expert") + lax.axis_index("expert")
    own_index = block * pair_count + jnp.arange(pair_count, dtype=jnp.int32)
    diagonal = (
        jnp.arange(all_images.shape[0], dtype=jnp.int32)[None, :] == own_index[:, None]
    ).astype(jnp.float32)
    coefs = (
        0.5 * (expscores / row_total[:, None] + expscores / col_total[None, :]) - diagonal
    ).astype(jnp.bfloat16)
    text_back = logit_scale * jnp.dot(coefs, all_images, preferred_element_type=jnp.float32)
    pooled_back = text_inverse * (
        text_back - text_unit * jnp.sum(text_unit * text_back, axis=1, keepdims=True)
    )
    layer_back = jnp.repeat(pooled_back / TEXT_LEN, TEXT_LEN, axis=0)
    gate_grad = jnp.sum(layer_back * expert_out, axis=1)
    out_back = (gate[:, None] * layer_back).astype(jnp.bfloat16)
    back_send = jnp.dot(table, out_back, preferred_element_type=jnp.float32).astype(jnp.bfloat16)
    received_back = lax.all_to_all(
        back_send.reshape(experts, capacity, width),
        "expert",
        split_axis=0,
        concat_axis=1,
        tiled=True,
    )
    grad_out = jnp.einsum(
        "erh,erd->ehd", activated, received_back, preferred_element_type=jnp.float32
    )
    act_back = jnp.einsum(
        "erd,ehd->erh", received_back, full_out, preferred_element_type=jnp.float32
    )
    pre_back = gelu_back(act_back)[0].astype(jnp.bfloat16)
    slots_back = jnp.einsum("erh,edh->erd", pre_back, full_in, preferred_element_type=jnp.float32)
    grad_in = jnp.einsum("erd,erh->edh", received, pre_back, preferred_element_type=jnp.float32)
    in_grad, out_grad = (
        lax.psum_scatter(
            grad_in.astype(jnp.bfloat16), "dp", scatter_dimension=1, tiled=True
        ).astype(jnp.float32),
        lax.psum_scatter(
            grad_out.astype(jnp.bfloat16), "dp", scatter_dimension=1, tiled=True
        ).astype(jnp.float32),
    )
    returned_back = lax.all_to_all(
        slots_back.astype(jnp.bfloat16), "expert", split_axis=1, concat_axis=0, tiled=True
    )
    normed_back = jnp.einsum(
        "st,sd->td",
        table,
        returned_back.reshape(experts * capacity, width),
        preferred_element_type=jnp.float32,
    )
    gained = normed_back * ln_gain
    token_back = layer_back + inverse * (
        gained
        - jnp.mean(gained, axis=1, keepdims=True)
        - scaled * jnp.mean(gained * scaled, axis=1, keepdims=True)
    )
    return (token_back.astype(jnp.bfloat16), gate_grad, in_grad, out_grad)


def solution(mesh):
    in_specs = (
        P(("dp", "expert"), None),
        P(("dp", "expert"), None),
        P(("dp", "expert")),
        P(),
        P("expert", "dp", None),
        P("expert", "dp", None),
        P(("dp", "expert"), None),
    )
    out_specs = (
        P(("dp", "expert"), None),
        P(("dp", "expert")),
        P("expert", "dp", None),
        P("expert", "dp", None),
    )
    return jax.shard_map(body, mesh=mesh, in_specs=in_specs, out_specs=out_specs, check_vma=False)
```

profile of v0, /device:TPU:1, one launch (start us, length us, event | category | flops | bytes accessed | tf_op | source)
XLA Modules:
  0.0 986.8 jit_solution(6844486432190048394)
XLA Ops:
  7.2 0.0 all-gather.4.cloned.1.call-start
  7.2 0.7 all-gather.4.cloned.1.call-update
  7.9 0.0 all-gather.6.cloned.1.call-start
  7.9 0.7 all-gather.6.cloned.1.call-update
  8.6 0.0 all-gather.8.cloned.1.call-start
  8.7 0.8 fusion.62
  9.5 1.4 fusion.63
  10.9 0.0 all-gather.8.cloned.1.call-update
  10.9 0.7 fusion.53
  11.7 0.2 reduce_window_sum.11
  11.9 0.8 select_reduce_fusion
  12.7 1.0 convert_reduce_fusion
  13.7 1.1 fusion.40
  14.9 0.7 compare_select_fusion
  15.6 1.2 convolution_convert_fusion.3
  16.8 0.1 reshape.204
  16.9 18.4 %all_to_all.16 = bf16[8,20,768]{2,1,0:T(8,128)(2,1)S(1)} all-to-all(bf16[8,20,768]{2,1,0:T(8,128)(2,1)S(1)} %reshape.204), channel_id=1, replica_groups=mesh['dp'=32,'expert'=8] {'expert'}, dimensions={0} | all-to-all | bytes 491520 | tf_op jit(solution)/shard_map/all_to_all | solution.py:49
  35.2 0.1 reshape.205
  35.3 0.0 copy-start.3
  35.3 96.3 %all-gather.4.cloned.1.call-done = bf16[1,768,3072]{2,1,0:T(8,128)(2,1)} async-done(((bf16[1,24,3072]{2,1,0:T(8,128)(2,1)}), bf16[1,768,3072]{2,1,0:T(8,128)(2,1)}) %all-gather.4.cloned.1.call-update) | async-done | bytes 4718608 | tf_op jit(solution)/shard_map/all_gather | solution.py:53
  131.6 9.1 multiply_convert_fusion
  140.7 105.0 %all-gather.6.cloned.1.call-done = bf16[1,3072,768]{2,1,0:T(8,128)(2,1)} async-done(((bf16[1,96,768]{2,1,0:T(8,128)(2,1)}), bf16[1,3072,768]{2,1,0:T(8,128)(2,1)}) %all-gather.6.cloned.1.call-update) | async-done | bytes 4718608 | tf_op jit(solution)/shard_map/all_gather | solution.py:54
  245.8 3.3 fusion.25
  249.0 0.0 copy-start.1
  249.0 0.0 copy-start.7
  249.1 0.4 copy.32
  249.4 0.5 broadcast.153
  250.0 2.1 reduce
  252.1 0.8 reshape.214
  252.8 5.5 all-to-all-start.1
  258.3 8.8 all-to-all-done.1
  267.2 0.2 reshape.215
  267.4 1.0 bitcast_reduce_fusion
  268.4 0.1 multiply_reduce_fusion.1
  268.5 82.3 %all-gather.8.cloned.1.call-done = bf16[2048,768]{1,0:T(8,128)(2,1)} async-done(((bf16[8,768]{1,0:T(8,128)(2,1)}), bf16[2048,768]{1,0:T(8,128)(2,1)}) %all-gather.8.cloned.1.call-update) | async-done | bytes 3145744 | tf_op jit(solution)/shard_map/all_gather | solution.py:77
  350.8 3.1 fusion.67
  353.9 76.8 %psum.7 = f32[2048]{0:T(1024)S(1)} all-reduce(f32[2048]{0:T(1024)S(1)} %get-tuple-element.7), channel_id=1, replica_groups=mesh['dp'=32,'expert'=8] {'dp','expert'}, use_global_device_ids=true, to_apply=%region_9.10 | all-reduce | flops 2048 | bytes 16384 | tf_op jit(solution)/shard_map/psum | solution.py:83
  430.7 0.7 multiply_reduce_fusion
  431.4 0.1 multiply_multiply_fusion.5
  431.4 0.1 fusion.41
  431.5 0.2 convolution_convert_fusion.2
  431.8 0.1 reshape.211
  431.8 13.5 %all_to_all.17 = bf16[8,20,768]{2,1,0:T(8,128)(2,1)S(1)} all-to-all(bf16[8,20,768]{2,1,0:T(8,128)(2,1)S(1)} %reshape.211), channel_id=1, replica_groups=mesh['dp'=32,'expert'=8] {'expert'}, dimensions={0} | all-to-all | bytes 491520 | tf_op jit(solution)/shard_map/all_to_all | solution.py:100
  445.3 0.1 reshape.212
  445.4 0.0 copy-start.4
  445.4 4.9 add_convert_fusion
  450.3 3.6 fusion.8
  453.9 0.0 reduce-scatter.3.cloned.1.call-update
  454.0 0.0 reduce-scatter.5.cloned.1.call-start
  454.0 1.1 copy-done.6
  455.1 3.7 fusion.9
  458.8 0.0 reduce-scatter.5.cloned.1.call-update
  458.9 4.0 fusion.28
  462.9 0.4 copy.31
  463.3 2.2 reduce.1
  465.5 0.1 reshape.216
  465.6 11.3 %all_to_all.18 = bf16[8,2,7680]{2,1,0:T(2,128)(2,1)S(1)} all-to-all(bf16[8,2,7680]{2,1,0:T(2,128)(2,1)S(1)} %reshape.216), channel_id=1, replica_groups=mesh['dp'=32,'expert'=8] {'expert'}, dimensions={0} | all-to-all | bytes 491520 | tf_op jit(solution)/shard_map/all_to_all | solution.py:124
  476.9 0.2 reshape.217
  477.1 0.4 fusion.66
  477.5 1.4 fusion.43
  478.9 234.4 %reduce-scatter.3.cloned.1.call-done = bf16[1,24,3072]{2,1,0:T(8,128)(2,1)} async-done(((bf16[1,768,3072]{2,1,0:T(8,128)(2,1)}), bf16[1,24,3072]{2,1,0:T(8,128)(2,1)}) %reduce-scatter.3.cloned.1.call-update) | async-done | bytes 147472 | tf_op jit(solution)/shard_map/reduce_scatter | solution.py:117
  713.4 1.6 convert_element_type.95
  715.0 263.6 %reduce-scatter.5.cloned.1.call-done = bf16[1,96,768]{2,1,0:T(8,128)(2,1)} async-done(((bf16[1,3072,768]{2,1,0:T(8,128)(2,1)}), bf16[1,96,768]{2,1,0:T(8,128)(2,1)}) %reduce-scatter.5.cloned.1.call-update) | async-done | bytes 147472 | tf_op jit(solution)/shard_map/reduce_scatter | solution.py:120
  978.7 1.6 convert_element_type.98
  (22 shorter events, 0.1 us)
Async XLA Ops:
  7.2 124.5 %all-gather.4.cloned.1.call-start = ((), (), s32[]{:S(2)}) async-start(), calls=%async_computation.6 | async-start | bytes 4866048 | tf_op jit(solution)/shard_map/all_gather | solution.py:53
  7.9 237.9 %all-gather.6.cloned.1.call-start = ((), (), s32[]{:S(2)}) async-start(), calls=%async_computation.7 | async-start | bytes 4866048 | tf_op jit(solution)/shard_map/all_gather | solution.py:54
  8.6 342.2 %all-gather.8.cloned.1.call-start = ((), (), s32[]{:S(2)}) async-start(), calls=%async_computation.8 | async-start | bytes 3158016 | tf_op jit(solution)/shard_map/all_gather | solution.py:77
  35.3 105.5 %copy-start.3 = (bf16[160,768]{1,0:T(8,128)(2,1)}, bf16[160,768]{1,0:T(8,128)(2,1)S(1)}, u32[]{:S(2)}) copy-start(bf16[160,768]{1,0:T(8,128)(2,1)S(1)} %reshape.205) | copy-start | bytes 737284
  140.7 105.0 %copy-start.5 = (bf16[160,3072]{1,0:T(8,128)(2,1)}, bf16[160,3072]{1,0:T(8,128)(2,1)S(1)}, u32[]{:S(2)}) copy-start(bf16[160,3072]{1,0:T(8,128)(2,1)S(1)} %get-tuple-element.8) | copy-start | bytes 2949124
  249.0 18.3 %copy-start.1 = (bf16[128,768]{1,0:T(8,128)(2,1)S(1)}, bf16[128,768]{1,0:T(8,128)(2,1)}, u32[]{:S(2)}) copy-start(bf16[128,768]{1,0:T(8,128)(2,1)} %param.7) | copy-start | bytes 589828
  249.0 18.3 %copy-start.7 = (f32[128]{0:T(128)S(1)}, f32[128]{0:T(128)}, u32[]{:S(2)}) copy-start(f32[128]{0:T(128)} %param.9) | copy-start | bytes 1540
  252.8 14.3 %all-to-all-start.1 = ((bf16[8,2,7680]{2,1,0:T(2,128)(2,1)}), bf16[8,2,7680]{2,1,0:T(2,128)(2,1)S(1)}, u32[]{:S(2)}, u32[]{:S(2)}) async-start(bf16[8,2,7680]{2,1,0:T(2,128)(2,1)} %reshape.214), calls=%async_computation.1 | async-start | bytes 491520 | tf_op jit(solution)/shard_map/all_to_all | solution.py:62
  258.3 455.1 %reduce-scatter.3.cloned.1.call-start = ((), (), s32[]{:S(2)}) async-start(), calls=%async_computation.9 | async-start | bytes 4866048 | tf_op jit(solution)/shard_map/reduce_scatter | solution.py:117
  350.8 79.8 %copy-start = (bf16[2048,768]{1,0:T(8,128)(2,1)S(1)}, bf16[2048,768]{1,0:T(8,128)(2,1)}, u32[]{:S(2)}) copy-start(bf16[2048,768]{1,0:T(8,128)(2,1)} %all-gather.8.cloned.1.call-done) | copy-start | bytes 9437188
  431.4 14.0 %copy-start.9 = (f32[160,3072]{1,0:T(8,128)S(1)}, f32[160,3072]{1,0:T(8,128)}, u32[]{:S(2)}) copy-start(f32[160,3072]{1,0:T(8,128)} %get-tuple-element.9) | copy-start | bytes 5898244
  445.4 5.0 copy-start.4
  453.9 1.2 copy-start.6
  454.0 524.7 %reduce-scatter.5.cloned.1.call-start = ((), (), s32[]{:S(2)}) async-start(), calls=%async_computation.10 | async-start | bytes 4866048 | tf_op jit(solution)/shard_map/reduce_scatter | solution.py:120
  462.9 14.2 %copy-start.8 = (f32[768]{0:T(1024)S(1)}, f32[768]{0:T(1024)}, u32[]{:S(2)}) copy-start(f32[768]{0:T(1024)} %param.10) | copy-start | bytes 9220
  462.9 14.6 %copy-start.2 = (f32[128,768]{1,0:T(8,128)S(1)}, f32[128,768]{1,0:T(8,128)}, u32[]{:S(2)}) copy-start(f32[128,768]{1,0:T(8,128)} %get-tuple-element.16) | copy-start | bytes 1179652
Sparse Core Ops, SparseCore 0:
  11.5 120.0 all-gather.3
  135.1 110.6 all-gather.5
  249.9 100.8 all-gather.7
  454.1 259.2 reduce-scatter.2
  718.8 259.8 reduce-scatter.4
where the time goes:
time: 988 us; the launch traced here: 987 us
  waiting for transfers between devices  792 us (80%)
  blocking collectives  120 us (12%)
  matrix products  35.2 us (4%)
  other arithmetic  16 us (2%)
  between operations  14 us (1%)
    reduce_scatter x1, waiting for transfers between devices, body(): lax.psum_scatter(grad_out.astype(jnp.bfloat16), 'dp', scatter_dimension=1...  264 us
    reduce_scatter x1, waiting for transfers between devices, body(): lax.psum_scatter(grad_in.astype(jnp.bfloat16), 'dp', scatter_dimension=1,...  234 us
    all_gather x1, waiting for transfers between devices, body(): lax.all_gather(w_out, 'dp', axis=1, tiled=True)  105 us
    all_gather x1, waiting for transfers between devices, body(): lax.all_gather(w_in, 'dp', axis=1, tiled=True)  96.3 us
    all_gather x1, waiting for transfers between devices, body(): lax.all_gather(image_norm, ('dp', 'expert'), axis=0, tiled=True)  82.3 us
    psum x1, blocking collectives, body(): col_total = lax.psum(jnp.sum(expscores, axis=0), ('dp', 'expert'))  76.8 us
  transfers between devices with their start and end apart: 6, of which 6 were waited for; matrix products, arithmetic and copies ran while one was open for 4% of the time, Pallas kernels for 0%

commit v1 on v0

v1 whole, which is shorter than its diff:
```python
import jax
import jax.numpy as jnp
from jax import lax
from jax.experimental import pallas as pl
from jax.experimental.pallas import tpu as pltpu
from jax.sharding import PartitionSpec as P

MESH = pl.DeviceIdType.MESH
F32 = jnp.float32
BF16 = jnp.bfloat16

D = 768
H = 3072
HALF = 1536
TOK = 128
CAP = 20
PAIR = 8
TEXT = 16
N = 16
R = 4
RO = 96
RI = 48
SLOTS = 320
SP = 384
EPS = 1e-6
SCALE = 100.0


def dot(a, b, ca=1, cb=0):
    return lax.dot_general(a, b, (((ca,), (cb,)), ((), ())), preferred_element_type=F32)


def iota(shape, axis):
    return lax.broadcasted_iota(jnp.int32, shape, axis)


def hot(mask):
    return jnp.where(mask, 1.0, 0.0).astype(BF16)


def split2(v):
    hi = v.astype(BF16)
    return hi, (v - hi.astype(F32)).astype(BF16)


def wrap(v):
    return lax.rem(v + 2 * R, R)


class Gather:
    def __init__(self, block, c1, c2, dev1, dev2, sem):
        self.block, self.c1, self.c2 = block, c1, c2
        self.dev1, self.dev2, self.sem = dev1, dev2, sem
        self.bs = [c1, wrap(c1 - 1), wrap(c1 + 1), wrap(c1 + 2)]

    def copy(self, k, ref, dev):
        return pltpu.make_async_remote_copy(
            src_ref=ref, dst_ref=ref, send_sem=self.sem.at[0, k], recv_sem=self.sem.at[1, k],
            device_id=dev, device_id_type=MESH,
        )

    def at(self, a, b, half=None):
        return self.block(wrap(a), wrap(b), half)

    def second(self, i):
        ref = self.at(self.bs[i], self.c2)
        self.copy(4 + 4 * i, ref, self.dev2(1)).start()
        self.copy(5 + 4 * i, ref, self.dev2(-1)).start()

    def start(self):
        ref = self.at(self.c1, self.c2)
        self.copy(0, ref, self.dev1(1)).start()
        self.copy(1, ref, self.dev1(-1)).start()
        self.second(0)

    def stage1(self):
        c1, c2 = self.c1, self.c2
        self.copy(0, self.at(c1 - 1, c2), self.dev1(1)).wait_recv()
        self.copy(2, self.at(c1 - 1, c2, 0), self.dev1(1)).start()
        self.second(1)
        self.copy(1, self.at(c1 + 1, c2), self.dev1(1)).wait_recv()
        self.copy(3, self.at(c1 + 1, c2, 1), self.dev1(-1)).start()
        self.second(2)

    def stage2(self):
        c1, c2 = self.c1, self.c2
        self.copy(2, self.at(c1 + 2, c2, 0), self.dev1(1)).wait_recv()
        self.copy(3, self.at(c1 + 2, c2, 1), self.dev1(1)).wait_recv()
        self.second(3)

    def stage3(self, i):
        b, c2 = self.bs[i], self.c2
        self.copy(4 + 4 * i, self.at(b, c2 - 1), self.dev2(1)).wait_recv()
        self.copy(6 + 4 * i, self.at(b, c2 - 1, 0), self.dev2(1)).start()
        self.copy(5 + 4 * i, self.at(b, c2 + 1), self.dev2(1)).wait_recv()
        self.copy(7 + 4 * i, self.at(b, c2 + 1, 1), self.dev2(-1)).start()

    def stage4(self):
        for i in range(4):
            self.copy(6 + 4 * i, self.at(self.bs[i], self.c2 + 2, 0), self.dev2(1)).wait_recv()
            self.copy(7 + 4 * i, self.at(self.bs[i], self.c2 + 2, 1), self.dev2(1)).wait_recv()

    def sent(self):
        c1, c2 = self.c1, self.c2
        for k in (0, 1):
            self.copy(k, self.at(c1, c2), self.dev1(1)).wait_send()
            self.copy(2 + k, self.at(c1, c2, k), self.dev1(1)).wait_send()
        for i in range(4):
            for k in (0, 1):
                self.copy(4 + 4 * i + k, self.at(c1, c2), self.dev1(1)).wait_send()
                self.copy(6 + 4 * i + k, self.at(c1, c2, k), self.dev1(1)).wait_send()


class Scatter:
    def __init__(self, block, c1, c2, dev1, dev2, halves, fulls, sem):
        self.block, self.c1, self.c2 = block, c1, c2
        self.dev1, self.dev2, self.sem = dev1, dev2, sem
        self.halves, self.fulls = halves, fulls
        self.bs = [wrap(c2 + 2), wrap(c2 + 1), wrap(c2 - 1), c2]

    def copy(self, k, src, dst, dev):
        return pltpu.make_async_remote_copy(
            src_ref=src, dst_ref=dst, send_sem=self.sem.at[0, k], recv_sem=self.sem.at[1, k],
            device_id=dev, device_id_type=MESH,
        )

    def at(self, a, b, half=None):
        return self.block(wrap(a), wrap(b), half)

    def add(self, ref, *others):
        total = ref[...].astype(F32)
        for other in others:
            total = total + other[...].astype(F32)
        ref[...] = total.astype(BF16)

    def start(self):
        for i in range(4):
            self.copy(4 * i, self.at(self.c1 + 2, self.bs[i], 0), self.halves.at[i, 0], self.dev1(1)).start()
            self.copy(4 * i + 1, self.at(self.c1 + 2, self.bs[i], 1), self.halves.at[i, 1], self.dev1(-1)).start()

    def got_half(self, i, k):
        ref = self.halves.at[i, k]
        self.copy(4 * i + k, ref, ref, self.dev1(1)).wait_recv()
        return ref

    def got_full(self, i, k):
        ref = self.fulls.at[i, k]
        self.copy(4 * i + 2 + k, ref, ref, self.dev1(1)).wait_recv()
        return ref

    def mid(self, i):
        b = self.bs[i]
        self.add(self.at(self.c1 + 1, b, 0), self.got_half(i, 0))
        self.copy(4 * i + 2, self.at(self.c1 + 1, b), self.fulls.at[i, 0], self.dev1(1)).start()
        self.add(self.at(self.c1 - 1, b, 1), self.got_half(i, 1))
        self.copy(4 * i + 3, self.at(self.c1 - 1, b), self.fulls.at[i, 1], self.dev1(-1)).start()

    def end(self, i):
        c1, b = self.c1, self.bs[i]
        first, second = self.got_full(i, 0), self.got_full(i, 1)
        if i == 0:
            self.add(self.at(c1, b), first, second)
            self.copy(16, self.at(c1, b, 0), self.halves.at[4, 0], self.dev2(1)).start()
            self.copy(17, self.at(c1, b, 1), self.halves.at[4, 1], self.dev2(-1)).start()
        elif i == 1:
            self.add(self.at(c1, b), first, second)
            self.add(self.at(c1, b, 0), self.got_half(4, 0))
            self.copy(18, self.at(c1, b), self.fulls.at[4, 0], self.dev2(1)).start()
        elif i == 2:
            self.add(self.at(c1, b), first, second)
            self.add(self.at(c1, b, 1), self.got_half(4, 1))
            self.copy(19, self.at(c1, b), self.fulls.at[4, 1], self.dev2(-1)).start()
        else:
            total = self.at(c1, b)[...].astype(F32) + first[...].astype(F32) + second[...].astype(F32)
            for k in (0, 1):
                total = total + self.got_full(4, k)[...].astype(F32)
            return total

    def sent(self):
        for i in range(5):
            for k in (0, 1):
                self.copy(4 * i + k, self.halves.at[i, k], self.halves.at[i, k], self.dev1(1)).wait_send()
                self.copy(4 * i + 2 + k, self.fulls.at[i, k], self.fulls.at[i, k], self.dev1(1)).wait_send()


def kernel(
    tok, ids, gate, gain, win, wout, img,
    tg, gg, dwin, dwout,
    sel, vsend, v32, v32b, full_in, full_out, img32, imgb,
    xsend, gsend, xr, gall, xs, xt, pre, cdf, act, actt, out32,
    contrib, crecv, tall, rsum, rrecv, csum, ccrecv, tb, tbrecv, lb, ob, pb,
    ggs, ggrecv, ib, ibrecv, gi, go, hi_buf, fi_buf, ho_buf, fo_buf,
    ag_i, ag_o, rs_i, rs_o, pair_sem, pair2_sem,
    s_img, s_x, s_g, s_c, s_t, s_r, s_cc, s_tb, s_lb, s_gg, s_ib,
):
    dp, ex = lax.axis_index("dp"), lax.axis_index("expert")
    xy, h = dp // 2, lax.rem(dp, 2)
    y, x = xy // R, lax.rem(xy, R)
    j = 8 * h + ex

    def z_dev(q):
        return (2 * xy + q // 8, lax.rem(q, 8))

    def p_dev(k):
        return (2 * k + h, ex)

    def x_dev(step):
        return p_dev(R * y + wrap(x + step))

    def y_dev(step):
        return p_dev(R * wrap(y + step) + x)

    def each(fn):
        def step(i, carry):
            fn(i)
            return carry

        lax.fori_loop(1, N, step, 0)

    class Exchange:
        def __init__(self, me, dev, src, dst, sem):
            self.me, self.dev, self.src, self.dst, self.sem = me, dev, src, dst, sem

        def copy(self, i, to, slot):
            return pltpu.make_async_remote_copy(
                src_ref=self.src(to), dst_ref=self.dst(slot), send_sem=self.sem.at[0, i], recv_sem=self.sem.at[1, i],
                device_id=self.dev(to), device_id_type=MESH,
            )

        def start(self):
            def go_on(i):
                self.copy(i, lax.rem(self.me + i, N), self.me).start()

            each(go_on)

        def wait(self):
            def go_on(i):
                self.copy(i, lax.rem(self.me + i, N), lax.rem(self.me + N - i, N)).wait_recv()

            each(go_on)

        def sent(self):
            def go_on(i):
                self.copy(i, lax.rem(self.me + i, N), self.me).wait_send()

            each(go_on)

    def rows(ref, k, n):
        return ref.at[pl.ds(pl.multiple_of(k * n, n), n)]

    barrier = pltpu.get_barrier_semaphore()

    def greet(i):
        pl.semaphore_signal(barrier, inc=1, device_id=z_dev(lax.rem(j + i, N)), device_id_type=MESH)
        pl.semaphore_signal(barrier, inc=1, device_id=p_dev(lax.rem(xy + i, N)), device_id_type=MESH)

    each(greet)

    rows(full_out, xy, RO)[...] = wout[...]
    source = iota((D, SP), 0)
    column = iota((D, SP), 1)
    spot = column + (column // RO) * RO
    sel[0] = hot(source == spot + RO * h)
    sel[1] = hot(source == spot + RO * (1 - h))
    mine = []
    for g in range(4):
        part = win[:, D * g : D * (g + 1)]
        mine.append(dot(part, sel[0]))
        vsend[:, SP * g : SP * (g + 1)] = dot(part, sel[1])
    image = img[...].astype(F32)
    image = image * lax.rsqrt(jnp.sum(image * image, axis=1, keepdims=True) + EPS)
    rows(img32, xy, PAIR)[...] = image.astype(BF16).astype(F32)

    pl.semaphore_wait(barrier, 2 * (N - 1))

    def out_at(buf):
        def block(xc, yc, half=None):
            row = pl.multiple_of((R * yc + xc) * RO, 32)
            if half is None:
                return buf.at[pl.ds(row, RO)]
            return buf.at[pl.ds(pl.multiple_of(row + 48 * half, 16), 48)]

        return block

    def in_at(buf):
        def block(xc, yc, half=None):
            row = pl.multiple_of((R * yc + xc) * RI, 16)
            if half is None:
                return buf.at[pl.ds(row, RI)]
            return buf.at[pl.ds(row, RI), pl.ds(D * half, D)]

        return block

    def swap(block):
        return lambda a, b, half=None: block(b, a, half)

    gather_out = Gather(out_at(full_out), x, y, x_dev, y_dev, ag_o)
    gather_in = Gather(swap(in_at(full_in)), y, x, y_dev, x_dev, ag_i)
    gather_out.start()

    other = (2 * xy + 1 - h, ex)
    pair = pltpu.make_async_remote_copy(
        src_ref=vsend, dst_ref=v32b, send_sem=pair_sem.at[0], recv_sem=pair_sem.at[1], device_id=other, device_id_type=MESH
    )
    pair.start()
    for g in range(4):
        v32[pl.ds(pl.multiple_of(24 * h, 8), 24), SP * g : SP * (g + 1)] = mine[g]

    images = Exchange(xy, p_dev, lambda q: rows(img32, xy, PAIR), lambda s: rows(img32, s, PAIR), s_img)
    images.start()

    inputs = tok[...].astype(F32)
    centred = inputs - jnp.mean(inputs, axis=1, keepdims=True)
    inverse = lax.rsqrt(jnp.mean(centred * centred, axis=1, keepdims=True) + EPS)
    normed = (centred * inverse * gain[...]).astype(BF16)
    token_sum = jnp.sum(inputs.reshape(PAIR, TEXT, D), axis=1)

    chosen = ids[...].astype(F32)
    lane = iota((TOK, TOK), 1).astype(F32)
    onehot = hot(lane == chosen)
    before = dot(hot(iota((TOK, TOK), 0) > iota((TOK, TOK), 1)), onehot)
    slot = jnp.sum(before * onehot.astype(F32), axis=1, keepdims=True)
    is_main = slot < 16.0
    is_extra = jnp.logical_and(slot >= 16.0, slot < float(CAP))
    main = hot(lane == jnp.where(is_main, 16.0 * chosen + slot, -1.0))
    extra = [hot(lane == jnp.where(is_extra, 16.0 * chosen + (4.0 * p - 16.0) + slot, -1.0)) for p in range(3)]
    jf = j.astype(F32)
    place = jnp.where(is_main, 16.0 * jf + slot, jnp.where(is_extra, 240.0 + 4.0 * jf + slot, -1.0))
    spots = hot(iota((TOK, SP), 1).astype(F32) == place)

    xsend[:, :D] = dot(main.T, normed).astype(BF16)
    tail = dot(extra[0].T, normed[:, 0:256]) + dot(extra[1].T, normed[:, 256:512]) + dot(extra[2].T, normed[:, 512:768])
    xsend[:, D:] = tail.astype(BF16)
    chosen_row = jnp.broadcast_to(chosen, (TOK, TOK)).T[: 8 * PAIR]
    row64 = iota((8 * PAIR, TOK), 0)
    lane64 = iota((8 * PAIR, TOK), 1)
    weight = jnp.where(
        jnp.logical_and(chosen_row == (row64 // PAIR).astype(F32), lane64 // TEXT == lax.rem(row64, PAIR)), gate[...], 0.0
    )
    w1 = weight.astype(BF16)
    w2, w3 = split2(weight - w1.astype(F32))
    gsend[...] = dot(w1, spots) + dot(w2, spots) + dot(w3, spots)

    send_x = Exchange(j, z_dev, lambda q: rows(xsend, lax.rem(q, 8), 16), lambda s: rows(xr, s, 16), s_x)
    send_g = Exchange(j, z_dev, lambda q: rows(gsend, lax.rem(q, 8), PAIR), lambda s: rows(gall, s, PAIR), s_g)
    send_x.start()
    send_g.start()
    rows(xr, j, 16)[...] = rows(xsend, ex, 16)[...]
    rows(gall, j, PAIR)[...] = rows(gsend, ex, PAIR)[...]

    gather_out.stage1()
    pair.wait_recv()
    v32[pl.ds(pl.multiple_of(24 * (1 - h), 8), 24), :] = v32b[...]
    rows(full_in, xy, RI)[...] = v32[...].astype(BF16)
    gather_in.start()
    gather_out.stage2()
    gather_out.stage3(0)
    gather_in.stage1()
    gather_out.stage3(1)
    gather_out.stage3(2)
    gather_in.stage2()
    gather_out.stage3(3)
    for i in range(4):
        gather_in.stage3(i)

    send_x.wait()
    send_g.wait()
    picked = [
        hot(iota((64, 256), 1) == 16 * (iota((64, 256), 0) // 4) + 4 * p + lax.rem(iota((64, 256), 0), 4)) for p in range(3)
    ]
    xs[0:256, :] = xr[:, :D]
    for p in range(3):
        xs[256:SLOTS, 256 * p : 256 * (p + 1)] = dot(picked[p], xr[:, D:]).astype(BF16)
    xs[SLOTS:, :] = jnp.zeros((SP - SLOTS, D), BF16)
    xt[...] = xs[...].T
    by_slot = gall[...].T
    gate_col = jnp.sum(by_slot, axis=1, keepdims=True)[:SLOTS]
    pair_of = hot(by_slot > 0.0)[:SLOTS]

    images.wait()
    imgb[...] = img32[...].astype(BF16)
    gather_in.stage4()

    def chunk(n, size):
        return pl.ds(pl.multiple_of(n * size, size), size)

    def forward(n, carry):
        cols = chunk(n, 256)
        value = dot(xs[0:SLOTS, :], full_in[:, cols])
        bell = 0.5 * (1.0 + lax.erf(value * (0.5**0.5)))
        pre[:, cols] = value
        cdf[:, cols] = bell
        act[0:SLOTS, cols] = (value * bell).astype(BF16)
        return carry

    lax.fori_loop(0, HALF // 256, forward, 0)
    act[SLOTS:, :] = jnp.zeros((SP - SLOTS, HALF), BF16)
    gather_out.stage4()

    def project(n, carry):
        cols = chunk(n, 256)
        out32[:, cols] = dot(act[0:SLOTS, :], full_out[:, cols])
        return carry

    lax.fori_loop(0, D // 256, project, 0)

    contrib[...] = dot(pair_of, (gate_col * out32[...]).astype(BF16), 0, 0)
    send_c = Exchange(j, z_dev, lambda q: rows(contrib, q, PAIR), lambda s: crecv.at[s], s_c)
    send_c.start()
    crecv[pl.ds(j, 1)] = rows(contrib, j, PAIR)[...].reshape(1, PAIR, D)

    def slope(n, carry):
        cols = chunk(n, 256)
        value = pre[:, cols]
        pre[:, cols] = cdf[:, cols] + value * (jnp.exp(-0.5 * value * value) * 0.3989422804014327)
        return carry

    lax.fori_loop(0, HALF // 256, slope, 0)

    send_c.wait()
    pooled = (token_sum + jnp.sum(crecv[...], axis=0)) * (1.0 / TEXT)
    q_inv = lax.rsqrt(jnp.sum(pooled * pooled, axis=1, keepdims=True) + EPS)
    unit = pooled * q_inv
    rows(tall, j, PAIR)[...] = unit.astype(BF16).astype(F32)
    send_t = Exchange(j, z_dev, lambda q: rows(tall, j, PAIR), lambda s: rows(tall, s, PAIR), s_t)
    send_t.start()
    actt[...] = act[...].T
    send_t.wait()

    scores = SCALE * dot(tall[...].astype(BF16), imgb[...], 1, 1)
    exped = jnp.exp(scores)
    csum[...] = jnp.broadcast_to(jnp.sum(exped, axis=0, keepdims=True), (8, TOK))
    rsum[...] = jnp.broadcast_to(jnp.sum(exped.T, axis=0, keepdims=True), (8, TOK))
    send_r = Exchange(j, z_dev, lambda q: rsum, lambda s: rrecv.at[s], s_r)
    send_cc = Exchange(xy, p_dev, lambda q: csum, lambda s: ccrecv.at[s], s_cc)
    send_r.start()
    send_cc.start()
    rrecv[pl.ds(j, 1)] = rsum[...].reshape(1, 8, TOK)
    ccrecv[pl.ds(xy, 1)] = csum[...].reshape(1, 8, TOK)
    text_at = iota((TOK, TOK), 0)
    image_at = iota((TOK, TOK), 1)
    diagonal = jnp.where(
        jnp.logical_and(image_at // PAIR == xy, text_at == PAIR * j + lax.rem(image_at, PAIR)), 1.0, 0.0
    )
    send_r.wait()
    send_cc.wait()
    row_total = jnp.broadcast_to(jnp.sum(rrecv[...], axis=0)[0:1], (TOK, TOK)).T
    col_total = jnp.sum(ccrecv[...], axis=0)[0:1]
    coefs = (0.5 * (exped / row_total + exped / col_total) - diagonal).astype(BF16)
    tb[...] = SCALE * dot(coefs, imgb[...])
    send_tb = Exchange(j, z_dev, lambda q: rows(tb, q, PAIR), lambda s: tbrecv.at[s], s_tb)
    send_tb.start()
    tbrecv[pl.ds(j, 1)] = rows(tb, j, PAIR)[...].reshape(1, PAIR, D)
    send_tb.wait()
    text_back = jnp.sum(tbrecv[...], axis=0)
    pooled_back = q_inv * (text_back - unit * jnp.sum(unit * text_back, axis=1, keepdims=True))
    layer_back = pooled_back * (1.0 / TEXT)
    rows(lb, j, PAIR)[...] = layer_back
    send_lb = Exchange(j, z_dev, lambda q: rows(lb, j, PAIR), lambda s: rows(lb, s, PAIR), s_lb)
    send_lb.start()
    send_lb.wait()

    lb_hi, lb_lo = split2(lb[...])
    slot_back = dot(pair_of, lb_hi) + dot(pair_of, lb_lo)
    ob[0:SLOTS, :] = (gate_col * slot_back).astype(BF16)
    ob[SLOTS:, :] = jnp.zeros((SP - SLOTS, D), BF16)
    pb[SLOTS:, :] = jnp.zeros((SP - SLOTS, HALF), BF16)

    def grad_out(n, carry):
        go[chunk(n, 256), :] = dot(actt[chunk(n, 256), :], ob[...]).astype(BF16)
        return carry

    lax.fori_loop(0, HALF // 256, grad_out, 0)
    scatter_out = Scatter(swap(out_at(go)), y, x, y_dev, x_dev, ho_buf, fo_buf, rs_o)
    scatter_out.start()

    def back(n, carry):
        cols = chunk(n, 256)
        act_back = dot(ob[0:SLOTS, :], full_out[cols, :], 1, 1)
        pb[0:SLOTS, cols] = (act_back * pre[:, cols]).astype(BF16)
        return carry

    lax.fori_loop(0, HALF // 256, back, 0)

    def grad_in(n, carry):
        cols = chunk(n, 256)
        gi[:, cols] = dot(xt[...], pb[:, cols]).astype(BF16)
        return carry

    lax.fori_loop(0, HALF // 256, grad_in, 0)
    scatter_in = Scatter(in_at(gi), x, y, x_dev, y_dev, hi_buf, fi_buf, rs_i)
    scatter_in.start()
    scatter_out.mid(0)

    gate_back = jnp.sum(slot_back * out32[...], axis=1, keepdims=True)
    gate_back = jnp.concatenate(
        [jnp.broadcast_to(gate_back, (SLOTS, TOK)), jnp.zeros((SP - SLOTS, TOK), F32)], axis=0
    )
    ggs[...] = gate_back.T[0:8]
    scatter_out.mid(1)

    spread = jnp.zeros((256, 256), F32)
    for p in range(3):
        cols = slice(256 * p, 256 * (p + 1))
        in_back = dot(pb[0:SLOTS, :], full_in[cols, :], 1, 1).astype(BF16)
        ib[:, cols] = in_back[0:256]
        spread = spread + dot(picked[p], in_back[256:SLOTS], 0, 0)
    ib[:, D:] = spread.astype(BF16)
    send_ib = Exchange(j, z_dev, lambda q: rows(ib, q, 16), lambda s: rows(ibrecv, s, 16), s_ib)
    send_gg = Exchange(j, z_dev, lambda q: ggs, lambda s: rows(ggrecv, s, 8), s_gg)
    send_ib.start()
    send_gg.start()
    rows(ibrecv, j, 16)[...] = rows(ib, j, 16)[...]
    rows(ggrecv, j, 8)[...] = ggs[...]

    scatter_in.mid(0)
    scatter_out.mid(2)
    scatter_in.mid(1)
    scatter_out.mid(3)
    scatter_in.mid(2)
    scatter_in.mid(3)
    scatter_out.end(0)
    scatter_in.end(0)
    scatter_out.end(1)
    scatter_in.end(1)
    scatter_out.end(2)
    scatter_in.end(2)

    send_ib.wait()
    send_gg.wait()
    inputs = tok[...].astype(F32)
    centred = inputs - jnp.mean(inputs, axis=1, keepdims=True)
    inverse = lax.rsqrt(jnp.mean(centred * centred, axis=1, keepdims=True) + EPS)
    scaled = centred * inverse
    back_main = dot(jnp.concatenate([main, main], axis=1), ibrecv[:, :D])
    back_tail = [dot(jnp.concatenate([e, e], axis=1), ibrecv[:, D:]) for e in extra]
    normed_back = back_main + jnp.concatenate(back_tail, axis=1)
    gained = normed_back * gain[...]
    repeated = jnp.broadcast_to(layer_back.reshape(PAIR, 1, D), (PAIR, TEXT, D)).reshape(TOK, D)
    tg[...] = (
        repeated
        + inverse * (gained - jnp.mean(gained, axis=1, keepdims=True) - scaled * jnp.mean(gained * scaled, axis=1, keepdims=True))
    ).astype(BF16)
    lane_i = iota((TOK, TOK), 1)
    owner = hot(
        jnp.logical_and(lax.rem(lane_i, 8) == 0, lax.rem(lane_i // 8, 8).astype(F32) == chosen)
    )
    got = ggrecv[...]
    g1 = got.astype(BF16)
    g2, g3 = split2(got - g1.astype(F32))
    gathered = dot(owner, g1) + dot(owner, g2) + dot(owner, g3)
    token_gate = jnp.sum(gathered * spots.astype(F32), axis=1, keepdims=True)
    gg[...] = jnp.broadcast_to(token_gate, (TOK, TOK)).T[0:1]

    vsum = scatter_in.end(3)
    v32[...] = vsum
    back_pair = pltpu.make_async_remote_copy(
        src_ref=v32.at[pl.ds(pl.multiple_of(24 * (1 - h), 8), 24)], dst_ref=v32b,
        send_sem=pair2_sem.at[0], recv_sem=pair2_sem.at[1], device_id=other, device_id_type=MESH,
    )
    back_pair.start()
    dwout[...] = scatter_out.end(3)
    kept = v32[pl.ds(pl.multiple_of(24 * h, 8), 24), :]
    held = []
    for g in range(4):
        hi, lo = split2(kept[:, SP * g : SP * (g + 1)])
        held.append(dot(hi, sel[0], 1, 1) + dot(lo, sel[0], 1, 1))
    back_pair.wait_recv()
    came = v32b[...]
    for g in range(4):
        hi, lo = split2(came[:, SP * g : SP * (g + 1)])
        dwin[:, D * g : D * (g + 1)] = held[g] + dot(hi, sel[1], 1, 1) + dot(lo, sel[1], 1, 1)

    pair.wait_send()
    back_pair.wait_send()
    gather_out.sent()
    gather_in.sent()
    scatter_out.sent()
    scatter_in.sent()
    for exchange in (images, send_x, send_g, send_c, send_t, send_r, send_cc, send_tb, send_lb, send_gg, send_ib):
        exchange.sent()


def body(tokens, expert_ids, gate, ln_gain, w_in, w_out, image_emb):
    vmem = pl.BlockSpec(memory_space=pltpu.VMEM)
    f32 = lambda *shape: pltpu.VMEM(shape, F32)
    b16 = lambda *shape: pltpu.VMEM(shape, BF16)
    sems = lambda *shape: pltpu.SemaphoreType.DMA(shape)
    token_grad, gate_grad, in_grad, out_grad = pl.pallas_call(
        kernel,
        out_shape=(
            jax.ShapeDtypeStruct((TOK, D), BF16),
            jax.ShapeDtypeStruct((1, TOK), F32),
            jax.ShapeDtypeStruct((24, H), F32),
            jax.ShapeDtypeStruct((RO, D), F32),
        ),
        in_specs=[vmem] * 7,
        out_specs=(vmem,) * 4,
        scratch_shapes=[
            b16(2, D, SP),
            f32(24, HALF),
            f32(RI, HALF),
            f32(24, HALF),
            b16(D, HALF),
            b16(HALF, D),
            f32(TOK, D),
            b16(TOK, D),
            b16(TOK, 1024),
            f32(64, SP),
            b16(256, 1024),
            f32(TOK, SP),
            b16(SP, D),
            b16(D, SP),
            f32(SLOTS, HALF),
            f32(SLOTS, HALF),
            b16(SP, HALF),
            b16(HALF, SP),
            f32(SLOTS, D),
            f32(TOK, D),
            f32(N, PAIR, D),
            f32(TOK, D),
            f32(8, TOK),
            f32(N, 8, TOK),
            f32(8, TOK),
            f32(N, 8, TOK),
            f32(TOK, D),
            f32(N, PAIR, D),
            f32(TOK, D),
            b16(SP, D),
            b16(SP, HALF),
            f32(8, SP),
            f32(TOK, SP),
            b16(256, 1024),
            b16(256, 1024),
            b16(D, HALF),
            b16(HALF, D),
            b16(5, 2, RI, D),
            b16(5, 2, RI, HALF),
            b16(5, 2, 48, D),
            b16(5, 2, RO, D),
            sems(2, 20),
            sems(2, 20),
            sems(2, 20),
            sems(2, 20),
            sems(2),
            sems(2),
        ]
        + [sems(2, N)] * 11,
        compiler_params=pltpu.CompilerParams(
            collective_id=0, has_side_effects=True, vmem_limit_bytes=56 * 1024 * 1024
        ),
        cost_estimate=pl.CostEstimate(flops=5_000_000_000, bytes_accessed=2_000_000, transcendentals=1_000_000),
    )(tokens, expert_ids, gate.reshape(1, TOK), ln_gain.reshape(1, D), w_in[0], w_out[0], image_emb)
    return token_grad, gate_grad.reshape(TOK), in_grad[None], out_grad[None]


def solution(mesh):
    in_specs = (
        P(("dp", "expert"), None),
        P(("dp", "expert"), None),
        P(("dp", "expert")),
        P(),
        P("expert", "dp", None),
        P("expert", "dp", None),
        P(("dp", "expert"), None),
    )
    out_specs = (
        P(("dp", "expert"), None),
        P(("dp", "expert")),
        P("expert", "dp", None),
        P("expert", "dp", None),
    )
    return jax.shard_map(body, mesh=mesh, in_specs=in_specs, out_specs=out_specs, check_vma=False)
```

time: 988 us -> 162 us (0.16)
  waiting for transfers between devices: 792 us -> 0 us
  Pallas kernels: 0 us -> 155 us
  blocking collectives: 120 us -> 0 us
  matrix products: 35.2 us -> 0 us
  other arithmetic: 16 us -> 0 us
  between operations: 14 us -> 0.67 us
    reduce_scatter x2 -> x0, waiting for transfers between devices: 498 us -> none  [the longest x1 264 us: body(): lax.psum_scatter(grad_out.astype(jnp.bfloat16), 'dp', scatter_dimension=1...]
    all_gather x3 -> x0, waiting for transfers between devices: 284 us -> none  [the longest x1 105 us: body(): lax.all_gather(w_out, 'dp', axis=1, tiled=True)]
    pallas_call x0 -> x1, Pallas kernels: none -> 155 us  [body(): pl.pallas_call(kernel, out_shape=(jax.ShapeDtypeStruct((TOK, D), BF16), j...]
    psum x1 -> x0, blocking collectives: 76.8 us -> none  [body(): col_total = lax.psum(jnp.sum(expscores, axis=0), ('dp', 'expert'))]
    all_to_all x3 -> x0, blocking collectives: 43.2 us -> none  [the longest x1 18.4 us: body(): lax.all_to_all(send.reshape(experts, capacity, width), 'expert', split_ax...]
    dot_general x12 -> x0, matrix products: 35.2 us -> none  [the longest x1 9.12 us: body(): jnp.einsum('erd,edh->erh', received, full_in, preferred_element_type=jnp....]
  transfers between devices with their start and end apart: 6 -> 0, of which waited for: 6 -> 0; matrix products, arithmetic and copies ran while one was open for 4% -> 0% of each run, Pallas kernels for 0% -> 0%
where the time goes in v1:
time: 162 us
  Pallas kernels  155 us (96%)
  local copies, waits for them, and re-layouts  6.04 us (4%)
    pallas_call x1, Pallas kernels, body(): pl.pallas_call(kernel, out_shape=(jax.ShapeDtypeStruct((TOK, D), BF16), j...  155 us
    unnamed x15, local copies, waits for them, and re-layouts  5.46 us

profile of v1, /device:TPU:1, one launch (start us, length us, event | category | flops | bytes accessed | tf_op | source)
XLA Modules:
  0.0 162.1 jit_solution(15527340925570079973)
XLA Ops:
  0.6 0.0 copy-start.2
  0.6 0.7 copy-done.2
  1.3 0.0 copy-start.3
  1.3 0.6 reshape.18.gain
  1.9 0.1 copy-done.3
  2.0 0.7 copy.11.ids
  2.7 155.4 %shard_map.102 = (bf16[128,768]{1,0:T(8,128)(2,1)}, f32[1,128]{1,0:T(1,128)}, f32[24,3072]{1,0:T(8,128)}, f32[96,768]{1,0:T(8,128)}) custom-call(bf16[128,768]{1,0:T(8,128)(2,1)} %tok.1, s32[128,1]{1,0:T(8,128)} %copy.11.ids, f32[1,128]{1,0:T(1,128)} %bitcast.10, f32[1,768]{1,0:T(1,128)} %reshape.18.gain, bf16[24,3072]{1,0:T(8,128)(2,1)} %bitcast.8, ...), custom_call_target="tpu_custom_call" | custom-call | flops 5000000000 | bytes 2000000 | tf_op jit(solution)/shard_map/pallas_call | solution.py:589
  158.1 0.0 copy-start.1
  158.1 0.0 copy-start.4
  158.1 1.7 %copy.16 = bf16[128,768]{1,0:T(8,128)(2,1)} copy(bf16[128,768]{1,0:T(8,128)(2,1)} %get-tuple-element.16) | data formatting | bytes 393216
  159.8 0.0 copy-done.4
  159.8 0.5 copy.17
  160.3 0.0 copy-done.1
  160.3 0.0 copy-start
  160.3 0.7 copy.18
  161.0 0.4 copy-done
  161.4 0.7 copy.19
Async XLA Ops:
  0.6 0.7 copy-start.2
  1.3 0.7 copy-start.3
  158.1 2.2 %copy-start.1 = (f32[24,3072]{1,0:T(8,128)S(1)}, f32[24,3072]{1,0:T(8,128)}, u32[]{:S(2)}) copy-start(f32[24,3072]{1,0:T(8,128)} %get-tuple-element.10) | copy-start | bytes 884740
  158.1 1.7 %copy-start.4 = (f32[1,128]{1,0:T(1,128)S(1)}, f32[1,128]{1,0:T(1,128)}, u32[]{:S(2)}) copy-start(f32[1,128]{1,0:T(1,128)} %get-tuple-element.9) | copy-start | bytes 1540
  160.3 1.1 copy-start

commit v2 on v1

v2 whole, which is shorter than its diff:
```python
import jax
import jax.numpy as jnp
from jax import lax
from jax.experimental import pallas as pl
from jax.experimental.pallas import tpu as pltpu
from jax.sharding import PartitionSpec as P

MESH = pl.DeviceIdType.MESH
F32 = jnp.float32
BF16 = jnp.bfloat16

D = 768
H = 3072
HALF = 1536
TOK = 128
CAP = 20
PAIR = 8
TEXT = 16
N = 16
R = 4
RO = 96
RI = 48
SLOTS = 320
SP = 384
EPS = 1e-6
SCALE = 100.0


def dot(a, b, ca=1, cb=0):
    return lax.dot_general(a, b, (((ca,), (cb,)), ((), ())), preferred_element_type=F32)


def iota(shape, axis):
    return lax.broadcasted_iota(jnp.int32, shape, axis)


def hot(mask):
    return jnp.where(mask, 1.0, 0.0).astype(BF16)


def split2(v):
    hi = v.astype(BF16)
    return hi, (v - hi.astype(F32)).astype(BF16)


def fold(v):
    m = v.shape[0] // 8
    v = v.reshape(m, 8, D)
    return jnp.concatenate([v[:, :, : D // 2], v[:, :, D // 2 :]], axis=1).reshape(16 * m, D // 2).astype(BF16)


def unfold(v):
    m = v.shape[0] // 16
    v = v.astype(F32).reshape(m, 16, D // 2)
    return jnp.concatenate([v[:, :8], v[:, 8:]], axis=2).reshape(8 * m, D)


def stack(v):
    return jnp.concatenate([v[:, :D], v[:, D:]], axis=0).astype(BF16)


def unstack(v):
    v = v.astype(F32)
    return jnp.concatenate([v[:24], v[24:]], axis=1)


def wrap(v):
    return lax.rem(v + 2 * R, R)


class Gather:
    def __init__(self, block, c1, c2, dev1, dev2, four, fifteen, sem, g):
        self.block, self.c1, self.c2 = block, c1, c2
        self.dev1, self.dev2, self.sem, self.g = dev1, dev2, sem, g
        self.four, self.fifteen = four, fifteen
        self.bs = [c1, wrap(c1 - 1), wrap(c1 + 1), wrap(c1 + 2)]

    def copy(self, k, ref, dev):
        return pltpu.make_async_remote_copy(
            src_ref=ref, dst_ref=ref, send_sem=self.sem.at[self.g, 12], recv_sem=self.sem.at[self.g, k],
            device_id=dev, device_id_type=MESH,
        )

    def got(self, k, ref):
        self.copy(k, ref, self.dev1(1)).wait_recv()
        return ref

    def at(self, a, b, half=None):
        return self.block(wrap(a), wrap(b), half)

    def second(self, i):
        ref = self.at(self.bs[i], self.c2)
        self.copy(3 + 2 * i, ref, self.dev2(1)).start()
        self.copy(4 + 2 * i, ref, self.dev2(-1)).start()

    def start(self):
        ref = self.at(self.c1, self.c2)
        self.copy(0, ref, self.dev1(1)).start()
        self.copy(1, ref, self.dev1(-1)).start()

    def stage1(self):
        c1, c2 = self.c1, self.c2
        self.got(0, self.at(c1 - 1, c2))
        self.copy(2, self.at(c1 - 1, c2, 0), self.dev1(1)).start()
        self.second(1)
        self.got(1, self.at(c1 + 1, c2))
        self.copy(2, self.at(c1 + 1, c2, 1), self.dev1(-1)).start()
        self.second(2)

    def stage2(self):
        self.got(2, self.at(self.c1 + 2, self.c2))
        self.second(3)

    def stage3(self, i):
        b, c2 = self.bs[i], self.c2
        self.got(3 + 2 * i, self.at(b, c2 - 1))
        self.copy(11, self.at(b, c2 - 1, 0), self.dev2(1)).start()
        self.got(4 + 2 * i, self.at(b, c2 + 1))
        self.copy(11, self.at(b, c2 + 1, 1), self.dev2(-1)).start()

    def stage4(self):
        self.got(11, self.four)

    def sent(self):
        self.copy(12, self.fifteen, self.dev1(1)).wait_send()


class Scatter:
    def __init__(self, block, c1, c2, dev1, dev2, halves, fulls, fifteen, sem, g):
        self.block, self.c1, self.c2 = block, c1, c2
        self.dev1, self.dev2, self.sem, self.g = dev1, dev2, sem, g
        self.halves, self.fulls, self.fifteen = halves.at[g], fulls.at[g], fifteen
        self.bs = [wrap(c2 + 2), wrap(c2 + 1), wrap(c2 - 1), c2]

    def copy(self, k, src, dst, dev):
        return pltpu.make_async_remote_copy(
            src_ref=src, dst_ref=dst, send_sem=self.sem.at[self.g, 15], recv_sem=self.sem.at[self.g, k],
            device_id=dev, device_id_type=MESH,
        )

    def got(self, k, ref):
        self.copy(k, ref, ref, self.dev1(1)).wait_recv()
        return ref

    def at(self, a, b, half=None):
        return self.block(wrap(a), wrap(b), half)

    def add(self, ref, *others):
        total = ref[...].astype(F32)
        for other in others:
            total = total + other[...].astype(F32)
        ref[...] = total.astype(BF16)

    def start(self):
        for i in range(4):
            self.copy(2 * i, self.at(self.c1 + 2, self.bs[i], 0), self.halves.at[i, 0], self.dev1(1)).start()
            self.copy(2 * i + 1, self.at(self.c1 + 2, self.bs[i], 1), self.halves.at[i, 1], self.dev1(-1)).start()

    def mid(self, i):
        b = self.bs[i]
        self.add(self.at(self.c1 + 1, b, 0), self.got(2 * i, self.halves.at[i, 0]))
        self.copy(8 + i, self.at(self.c1 + 1, b), self.fulls.at[i, 0], self.dev1(1)).start()
        self.add(self.at(self.c1 - 1, b, 1), self.got(2 * i + 1, self.halves.at[i, 1]))
        self.copy(8 + i, self.at(self.c1 - 1, b), self.fulls.at[i, 1], self.dev1(-1)).start()

    def end(self, i):
        c1, b = self.c1, self.bs[i]
        self.got(8 + i, self.fulls.at[i])
        first, second = self.fulls.at[i, 0], self.fulls.at[i, 1]
        if i == 0:
            self.add(self.at(c1, b), first, second)
            self.copy(12, self.at(c1, b, 0), self.halves.at[4, 0], self.dev2(1)).start()
            self.copy(13, self.at(c1, b, 1), self.halves.at[4, 1], self.dev2(-1)).start()
        elif i == 1:
            self.add(self.at(c1, b), first, second)
            self.add(self.at(c1, b, 0), self.got(12, self.halves.at[4, 0]))
            self.copy(14, self.at(c1, b), self.fulls.at[4, 0], self.dev2(1)).start()
        elif i == 2:
            self.add(self.at(c1, b), first, second)
            self.add(self.at(c1, b, 1), self.got(13, self.halves.at[4, 1]))
            self.copy(14, self.at(c1, b), self.fulls.at[4, 1], self.dev2(-1)).start()
        else:
            total = self.at(c1, b)[...].astype(F32) + first[...].astype(F32) + second[...].astype(F32)
            self.got(14, self.fulls.at[4])
            for k in (0, 1):
                total = total + self.fulls[4, k].astype(F32)
            return total

    def sent(self):
        self.copy(15, self.fifteen, self.fifteen, self.dev1(1)).wait_send()


def kernel(
    tok, ids, gate, gain, win, wout, img,
    tg, gg, dwin, dwout,
    sel, vsend, v32, vcame, vback, vfinal, full_in, full_out, imgs, imgb,
    xsend, xr, xs, xt, pre, cdf, act, actt, out32,
    contrib, cjoin, csend, crecv, tall, rsum, rrecv, csum, ccrecv, tb, tbrecv, lb, ob, pb,
    ib, ibrecv, gi, go, halves, fulls,
    ag_sem, rs_sem, pair_sem, pair2_sem,
    s_img, s_x, s_c, s_t, s_r, s_cc, s_tb, s_lb, s_ib, s_join, s_share,
):
    dp, ex = lax.axis_index("dp"), lax.axis_index("expert")
    xy, h = dp // 2, lax.rem(dp, 2)
    y, x = xy // R, lax.rem(xy, R)
    j = 8 * h + ex

    def z_dev(q):
        return (2 * xy + q // 8, lax.rem(q, 8))

    def p_dev(k):
        return (2 * k + h, ex)

    chip, core = 4 * h + ex // 2, lax.rem(ex, 2)
    seat = 8 * core + chip

    def c_dev(k):
        return (2 * xy + k // 4, 2 * lax.rem(k, 4) + core)

    twin = (dp, ex + 1 - 2 * core)

    def x_dev(step):
        return p_dev(R * y + wrap(x + step))

    def y_dev(step):
        return p_dev(R * wrap(y + step) + x)

    def each(fn):
        def step(i, carry):
            fn(i)
            return carry

        lax.fori_loop(1, N, step, 0)

    class Exchange:
        def __init__(self, me, dev, src, dst, all_but_one, sem, size=N):
            self.me, self.dev, self.src, self.dst, self.sem = me, dev, src, dst, sem
            self.all_but_one, self.size = all_but_one, size

        def copy(self, src, dst, to):
            return pltpu.make_async_remote_copy(
                src_ref=src, dst_ref=dst, send_sem=self.sem.at[0], recv_sem=self.sem.at[1],
                device_id=self.dev(to), device_id_type=MESH,
            )

        def start(self):
            def step(i, carry):
                to = lax.rem(self.me + i, self.size)
                self.copy(self.src(to), self.dst(self.me), to).start()
                return carry

            lax.fori_loop(1, self.size, step, 0)

        def wait(self):
            self.copy(self.all_but_one, self.all_but_one, lax.rem(self.me + 1, self.size)).wait_recv()

        def sent(self):
            self.copy(self.all_but_one, self.all_but_one, lax.rem(self.me + 1, self.size)).wait_send()

    def rows(ref, k, n):
        return ref.at[pl.ds(pl.multiple_of(k * n, n), n)]

    barrier = pltpu.get_barrier_semaphore()

    def greet(i):
        pl.semaphore_signal(barrier, inc=1, device_id=z_dev(lax.rem(j + i, N)), device_id_type=MESH)
        pl.semaphore_signal(barrier, inc=1, device_id=p_dev(lax.rem(xy + i, N)), device_id_type=MESH)

    each(greet)

    rows(full_out, xy, RO)[...] = wout[...]
    source = iota((D, SP), 0)
    column = iota((D, SP), 1)
    spot = column + (column // RO) * RO
    sel[0] = hot(source == spot + RO * h)
    sel[1] = hot(source == spot + RO * (1 - h))
    mine, theirs = [], []
    for g in range(4):
        part = win[:, D * g : D * (g + 1)]
        mine.append(dot(part, sel[0]))
        theirs.append(dot(part, sel[1]))
    vsend[...] = stack(jnp.concatenate(theirs, axis=1))
    for g in range(4):
        v32[pl.ds(pl.multiple_of(24 * h, 8), 24), SP * g : SP * (g + 1)] = mine[g]
    image = img[...].astype(F32)
    image = image * lax.rsqrt(jnp.sum(image * image, axis=1, keepdims=True) + EPS)
    rows(imgs, j, 16)[...] = fold(image)

    inputs = tok[...].astype(F32)
    centred = inputs - jnp.mean(inputs, axis=1, keepdims=True)
    inverse = lax.rsqrt(jnp.mean(centred * centred, axis=1, keepdims=True) + EPS)
    normed = (centred * inverse * gain[...].reshape(1, D)).astype(BF16)
    token_sum = jnp.sum(inputs.reshape(PAIR, TEXT, D), axis=1)

    chosen_row = jnp.broadcast_to(ids[...].astype(F32), (TOK, TOK))
    chosen = chosen_row.T[:, 0:1]
    lane = iota((TOK, TOK), 1).astype(F32)
    onehot = hot(lane == chosen)
    before = dot(hot(iota((TOK, TOK), 0) > iota((TOK, TOK), 1)), onehot)
    slot = jnp.sum(before * onehot.astype(F32), axis=1, keepdims=True)
    is_main = slot < 16.0
    is_extra = jnp.logical_and(slot >= 16.0, slot < float(CAP))
    main = hot(lane == jnp.where(is_main, 16.0 * chosen + slot, -1.0))
    extra = [hot(lane == jnp.where(is_extra, 16.0 * chosen + (4.0 * p - 16.0) + slot, -1.0)) for p in range(3)]
    at_slot = iota((TOK, 256), 1).astype(F32) == jnp.where(slot < float(CAP), slot, -1.0)

    xsend[:, :D] = dot(main.T, normed).astype(BF16)
    tail = dot(extra[0].T, normed[:, 0:256]) + dot(extra[1].T, normed[:, 256:512]) + dot(extra[2].T, normed[:, 512:768])
    gate_row = gate[...]
    gate1 = gate_row.astype(BF16).astype(F32)
    gate2 = (gate_row - gate1).astype(BF16).astype(F32)
    gate3 = gate_row - gate1 - gate2
    line = iota((TOK, TOK), 0)
    kind = lax.rem(line, 16)
    pair_row = (iota((TOK, TOK), 1) // TEXT).astype(F32)
    notes = jnp.where(kind == 12, gate1, jnp.where(kind == 13, gate2, jnp.where(kind == 14, gate3, jnp.where(kind == 15, pair_row, 0.0))))
    notes = jnp.where((line // 16).astype(F32) == chosen_row, notes, 0.0)
    xsend[:, D:] = (tail + dot(notes.astype(BF16), hot(at_slot))).astype(BF16)
    rows(xr, j, 16)[...] = rows(xsend, ex, 16)[...]

    pl.semaphore_wait(barrier, 2 * (N - 1))

    def out_at(buf, part):
        def block(xc, yc, half=None):
            row = pl.multiple_of((R * yc + xc) * RO + 48 * part, 16)
            if half is None:
                return buf.at[pl.ds(row, 48)]
            return buf.at[pl.ds(row, 48), pl.ds(SP * half, SP)]

        return block

    def in_at(buf, part):
        def block(xc, yc, half=None):
            row = pl.multiple_of((R * yc + xc) * RI, 16)
            if half is None:
                return buf.at[pl.ds(row, RI), pl.ds(D * part, D)]
            return buf.at[pl.ds(row, RI), pl.ds(D * part + SP * half, SP)]

        return block

    def both(make, buf, at, first, *args):
        other_way = at(buf, 1)
        return (
            make(at(buf, 0), x, y, x_dev, y_dev, *args, first),
            make(lambda a, b, half=None: other_way(b, a, half), y, x, y_dev, x_dev, *args, first + 1),
        )

    fifteen = full_out.at[pl.ds(0, 15 * 48)]
    outs = both(Gather, full_out, out_at, 0, full_out.at[pl.ds(0, 192)], fifteen, ag_sem)
    ins = both(Gather, full_in, in_at, 2, full_in.at[pl.ds(0, 96)], fifteen, ag_sem)

    other = (2 * xy + 1 - h, ex)
    pair = pltpu.make_async_remote_copy(
        src_ref=vsend, dst_ref=vcame, send_sem=pair_sem.at[0], recv_sem=pair_sem.at[1], device_id=other, device_id_type=MESH
    )
    pair.start()
    for part in outs:
        part.start()
    for part in outs:
        part.second(0)

    images = Exchange(j, z_dev, lambda q: rows(imgs, j, 16), lambda s: rows(imgs, s, 16), imgs.at[pl.ds(0, 240)], s_img)
    images.start()

    send_x = Exchange(j, z_dev, lambda q: rows(xsend, lax.rem(q, 8), 16), lambda s: rows(xr, s, 16), xr.at[pl.ds(0, 240)], s_x)
    send_x.start()

    for part in outs:
        part.stage1()
    for part in outs:
        part.stage2()
    for part in outs:
        part.stage3(0)
    pair.wait_recv()
    v32[pl.ds(pl.multiple_of(24 * (1 - h), 8), 24), :] = unstack(vcame[...])
    rows(full_in, xy, RI)[...] = v32[...].astype(BF16)
    for part in ins:
        part.start()
    for part in ins:
        part.second(0)
    for i in (1, 2):
        for part in outs:
            part.stage3(i)
    for part in ins:
        part.stage1()
    for part in outs:
        part.stage3(3)
    for part in ins:
        part.stage2()
    for i in range(4):
        for part in ins:
            part.stage3(i)

    send_x.wait()
    row64 = iota((64, 256), 0)
    lane64 = iota((64, 256), 1)
    picked = [hot(lane64 == 16 * (row64 // 4) + 4 * p + lax.rem(row64, 4)) for p in range(3)]
    xs[0:256, :] = xr[:, :D]
    for p in range(3):
        xs[256:SLOTS, 256 * p : 256 * (p + 1)] = dot(picked[p], xr[:, D:]).astype(BF16)
    xs[SLOTS:, :] = jnp.zeros((SP - SLOTS, D), BF16)
    xt[...] = xs[...].T
    slot_i = iota((SLOTS, 256), 0)
    lane_i = iota((SLOTS, 256), 1)
    slot_from = jnp.where(slot_i < 256, slot_i // 16, (slot_i - 256) // 4)
    slot_at = jnp.where(slot_i < 256, lax.rem(slot_i, 16), 16 + lax.rem(slot_i, 4))
    note_of = [hot(lane_i == 16 * slot_from + 12 + m) for m in range(4)]
    tails = xr[:, D:]
    own_lane = lane_i == slot_at
    gate_col = jnp.sum(jnp.where(own_lane, dot(note_of[0] + note_of[1] + note_of[2], tails), 0.0), axis=1, keepdims=True)
    pair_col = jnp.sum(jnp.where(own_lane, dot(note_of[3], tails), 0.0), axis=1, keepdims=True)
    first_pair = (PAIR * (8 * lax.rem(slot_from, 2) + slot_from // 2))[:, :TOK].astype(F32)
    pair_of = hot(lane_i[:, :TOK].astype(F32) == first_pair + pair_col)

    images.wait()
    imgb[...] = unfold(imgs[...]).astype(BF16)
    for part in ins:
        part.stage4()

    def chunk(n, size):
        return pl.ds(pl.multiple_of(n * size, size), size)

    def forward(n, carry):
        cols = chunk(n, 256)
        value = dot(xs[0:SLOTS, :], full_in[:, cols])
        bell = 0.5 * (1.0 + lax.erf(value * (0.5**0.5)))
        pre[:, cols] = value
        cdf[:, cols] = bell
        act[0:SLOTS, cols] = (value * bell).astype(BF16)
        return carry

    lax.fori_loop(0, HALF // 256, forward, 0)
    act[SLOTS:, :] = jnp.zeros((SP - SLOTS, HALF), BF16)
    for part in outs:
        part.stage4()

    def project(n, carry):
        cols = chunk(n, 256)
        out32[:, cols] = dot(act[0:SLOTS, :], full_out[:, cols])
        return carry

    lax.fori_loop(0, D // 256, project, 0)

    contrib[...] = fold(dot(pair_of, (gate_col * out32[...]).astype(BF16), 0, 0))
    join = pltpu.make_async_remote_copy(
        src_ref=rows(contrib, 1 - core, 128), dst_ref=cjoin, send_sem=s_join.at[0], recv_sem=s_join.at[1],
        device_id=twin, device_id_type=MESH,
    )
    join.start()
    join.wait_recv()
    joined = rows(contrib, core, 128)
    csend[...] = (joined[...].astype(F32) + cjoin[...].astype(F32)).astype(BF16)
    send_c = Exchange(
        chip, c_dev, lambda q: rows(csend, q, 16), lambda s: rows(crecv, s, 16), crecv.at[pl.ds(0, 112)], s_c, 8
    )
    send_c.start()
    rows(crecv, chip, 16)[...] = rows(csend, chip, 16)[...]

    def slope(n, carry):
        cols = chunk(n, 256)
        value = pre[:, cols]
        pre[:, cols] = cdf[:, cols] + value * (jnp.exp(-0.5 * value * value) * 0.3989422804014327)
        return carry

    lax.fori_loop(0, HALF // 256, slope, 0)

    send_c.wait()
    pooled = (token_sum + jnp.sum(unfold(crecv[...]).reshape(8, PAIR, D), axis=0)) * (1.0 / TEXT)
    q_inv = lax.rsqrt(jnp.sum(pooled * pooled, axis=1, keepdims=True) + EPS)
    unit = pooled * q_inv
    rows(tall, xy, 16)[...] = fold(unit)
    send_t = Exchange(xy, p_dev, lambda q: rows(tall, xy, 16), lambda s: rows(tall, s, 16), tall.at[pl.ds(0, 240)], s_t)
    send_t.start()
    actt[...] = act[...].T
    send_t.wait()

    scores = SCALE * dot(unfold(tall[...]).astype(BF16), imgb[...], 1, 1)
    exped = jnp.exp(scores)
    csum[...] = jnp.sum(exped, axis=0, keepdims=True)
    rsum[...] = jnp.sum(exped.T, axis=0, keepdims=True)
    send_r = Exchange(xy, p_dev, lambda q: rsum, lambda s: rrecv.at[s], rrecv.at[pl.ds(0, N - 1)], s_r)
    send_cc = Exchange(j, z_dev, lambda q: csum, lambda s: ccrecv.at[s], ccrecv.at[pl.ds(0, N - 1)], s_cc)
    send_r.start()
    send_cc.start()
    rrecv[pl.ds(xy, 1)] = rsum[...].reshape(1, 1, TOK)
    ccrecv[pl.ds(j, 1)] = csum[...].reshape(1, 1, TOK)
    text_at = iota((TOK, TOK), 0)
    image_at = iota((TOK, TOK), 1)
    diagonal = jnp.where(
        jnp.logical_and(image_at // PAIR == j, text_at == PAIR * xy + lax.rem(image_at, PAIR)), 1.0, 0.0
    )
    send_r.wait()
    send_cc.wait()
    row_total = jnp.broadcast_to(jnp.sum(rrecv[...], axis=0), (TOK, TOK)).T
    col_total = jnp.sum(ccrecv[...], axis=0)
    coefs = (0.5 * (exped / row_total + exped / col_total) - diagonal).astype(BF16)
    tb[...] = fold(SCALE * dot(coefs, imgb[...]))
    send_tb = Exchange(xy, p_dev, lambda q: rows(tb, q, 16), lambda s: rows(tbrecv, s, 16), tbrecv.at[pl.ds(0, 240)], s_tb)
    send_tb.start()
    rows(tbrecv, xy, 16)[...] = rows(tb, xy, 16)[...]
    send_tb.wait()
    text_back = jnp.sum(unfold(tbrecv[...]).reshape(N, PAIR, D), axis=0)
    pooled_back = q_inv * (text_back - unit * jnp.sum(unit * text_back, axis=1, keepdims=True))
    layer_back = pooled_back * (1.0 / TEXT)
    rows(lb, seat, 16)[...] = fold(layer_back)
    send_lb = Exchange(
        chip, c_dev, lambda q: rows(lb, seat, 16), lambda s: rows(lb, 8 * core + s, 16), lb.at[pl.ds(0, 112)], s_lb, 8
    )
    send_lb.start()
    send_lb.wait()
    ours = rows(lb, core, 128)
    share = pltpu.make_async_remote_copy(
        src_ref=ours, dst_ref=ours, send_sem=s_share.at[0], recv_sem=s_share.at[1], device_id=twin, device_id_type=MESH
    )
    share.start()
    share.wait_recv()

    slot_back = dot(pair_of, unfold(lb[...]).astype(BF16))
    ob[0:SLOTS, :] = (gate_col * slot_back).astype(BF16)
    ob[SLOTS:, :] = jnp.zeros((SP - SLOTS, D), BF16)
    pb[SLOTS:, :] = jnp.zeros((SP - SLOTS, HALF), BF16)

    def back(n, carry):
        cols = chunk(n, 256)
        act_back = dot(ob[0:SLOTS, :], full_out[cols, :], 1, 1)
        pb[0:SLOTS, cols] = (act_back * pre[:, cols]).astype(BF16)
        return carry

    def grad_in(n, carry):
        cols = chunk(n, 256)
        gi[:, cols] = dot(xt[...], pb[:, cols]).astype(BF16)
        return carry

    def grad_out(n, carry):
        go[chunk(n, 256), :] = dot(actt[chunk(n, 256), :], ob[...]).astype(BF16)
        return carry

    s_ins = both(Scatter, gi, in_at, 0, halves, fulls, fifteen, rs_sem)
    s_outs = both(Scatter, go, out_at, 2, halves, fulls, fifteen, rs_sem)
    for k in (0, 1):
        lax.fori_loop(3 * k, 3 * k + 3, back, 0)
        lax.fori_loop(3 * k, 3 * k + 3, grad_in, 0)
        s_ins[k].start()

    lax.fori_loop(0, HALF // 256, grad_out, 0)
    for part in s_outs:
        part.start()

    gate_back = jnp.sum(slot_back * out32[...], axis=1, keepdims=True)
    back1 = gate_back.astype(BF16).astype(F32)
    back2 = (gate_back - back1).astype(BF16).astype(F32)
    backs = [back1, back2, gate_back - back1 - back2]
    spread = jnp.zeros((256, 256), F32)
    for m in range(3):
        spread = spread + dot(note_of[m], jnp.where(own_lane, backs[m], 0.0).astype(BF16), 0, 0)
    for p in range(3):
        cols = slice(256 * p, 256 * (p + 1))
        in_back = dot(pb[0:SLOTS, :], full_in[cols, :], 1, 1).astype(BF16)
        ib[:, cols] = in_back[0:256]
        spread = spread + dot(picked[p], in_back[256:SLOTS], 0, 0)
    ib[:, D:] = spread.astype(BF16)
    send_ib = Exchange(j, z_dev, lambda q: rows(ib, q, 16), lambda s: rows(ibrecv, s, 16), ibrecv.at[pl.ds(0, 240)], s_ib)
    send_ib.start()
    rows(ibrecv, j, 16)[...] = rows(ib, j, 16)[...]

    for i in range(4):
        for part in s_ins:
            part.mid(i)
    for i in range(3):
        for part in s_ins:
            part.end(i)
        for part in s_outs:
            part.mid(i)
    v32[...] = jnp.concatenate([part.end(3) for part in s_ins], axis=1)
    vback[...] = stack(v32[pl.ds(pl.multiple_of(24 * (1 - h), 8), 24), :])
    back_pair = pltpu.make_async_remote_copy(
        src_ref=vback, dst_ref=vfinal,
        send_sem=pair2_sem.at[0], recv_sem=pair2_sem.at[1], device_id=other, device_id_type=MESH,
    )
    back_pair.start()
    for part in s_outs:
        part.mid(3)
    for i in range(2):
        for part in s_outs:
            part.end(i)

    send_ib.wait()
    inputs = tok[...].astype(F32)
    centred = inputs - jnp.mean(inputs, axis=1, keepdims=True)
    inverse = lax.rsqrt(jnp.mean(centred * centred, axis=1, keepdims=True) + EPS)
    scaled = centred * inverse
    back_main = dot(jnp.concatenate([main, main], axis=1), ibrecv[:, :D])
    back_tail = [dot(jnp.concatenate([e, e], axis=1), ibrecv[:, D:]) for e in extra]
    normed_back = back_main + jnp.concatenate(back_tail, axis=1)
    gained = normed_back * gain[...].reshape(1, D)
    repeated = jnp.broadcast_to(layer_back.reshape(PAIR, 1, D), (PAIR, TEXT, D)).reshape(TOK, D)
    tg[...] = (
        repeated
        + inverse * (gained - jnp.mean(gained, axis=1, keepdims=True) - scaled * jnp.mean(gained * scaled, axis=1, keepdims=True))
    ).astype(BF16)
    row_i = iota((TOK, 256), 1)
    kind = lax.rem(row_i, 16)
    owner = jnp.logical_and(jnp.logical_and(kind >= 12, kind < 15), lax.rem(row_i // 16, 8).astype(F32) == chosen)
    gathered = dot(hot(owner), ibrecv[:, D:])
    token_gate = jnp.sum(jnp.where(at_slot, gathered, 0.0), axis=1, keepdims=True)
    gg[...] = jnp.broadcast_to(token_gate, (TOK, TOK)).T[0:1]

    for part in s_outs:
        part.end(2)
    for k in (0, 1):
        dwout[48 * k : 48 * (k + 1), :] = s_outs[k].end(3)
    kept = v32[pl.ds(pl.multiple_of(24 * h, 8), 24), :]
    held = []
    for g in range(4):
        hi, lo = split2(kept[:, SP * g : SP * (g + 1)])
        held.append(dot(hi, sel[0], 1, 1) + dot(lo, sel[0], 1, 1))
    back_pair.wait_recv()
    came = unstack(vfinal[...])
    for g in range(4):
        dwin[:, D * g : D * (g + 1)] = held[g] + dot(came[:, SP * g : SP * (g + 1)].astype(BF16), sel[1], 1, 1)

    pair.wait_send()
    join.wait_send()
    share.wait_send()
    back_pair.wait_send()
    for part in outs + ins + s_ins + s_outs:
        part.sent()
    for exchange in (images, send_x, send_c, send_t, send_r, send_cc, send_tb, send_lb, send_ib):
        exchange.sent()


def hand_on(*refs):
    for k in range(4):
        refs[4 + k][...] = refs[k][...]


def body(tokens, expert_ids, gate, ln_gain, w_in, w_out, image_emb):
    vmem = pl.BlockSpec(memory_space=pltpu.VMEM)
    f32 = lambda *shape: pltpu.VMEM(shape, F32)
    b16 = lambda *shape: pltpu.VMEM(shape, BF16)
    sems = lambda *shape: pltpu.SemaphoreType.DMA(shape)
    token_grad, gate_grad, in_grad, out_grad = pl.pallas_call(
        kernel,
        out_shape=(
            jax.ShapeDtypeStruct((TOK, D), BF16),
            jax.ShapeDtypeStruct((1, TOK), F32),
            jax.ShapeDtypeStruct((24, H), F32),
            jax.ShapeDtypeStruct((RO, D), F32),
        ),
        in_specs=[vmem] * 7,
        out_specs=(vmem,) * 4,
        scratch_shapes=[
            b16(2, D, SP),
            b16(RI, D),
            f32(RI, HALF),
            b16(RI, D),
            b16(RI, D),
            b16(RI, D),
            b16(D, HALF),
            b16(HALF, D),
            b16(256, D // 2),
            b16(TOK, D),
            b16(TOK, 1024),
            b16(256, 1024),
            b16(SP, D),
            b16(D, SP),
            f32(SLOTS, HALF),
            f32(SLOTS, HALF),
            b16(SP, HALF),
            b16(HALF, SP),
            f32(SLOTS, D),
            b16(256, D // 2),
            b16(128, D // 2),
            b16(128, D // 2),
            b16(128, D // 2),
            b16(256, D // 2),
            f32(1, TOK),
            f32(N, 1, TOK),
            f32(1, TOK),
            f32(N, 1, TOK),
            b16(256, D // 2),
            b16(256, D // 2),
            b16(256, D // 2),
            b16(SP, D),
            b16(SP, HALF),
            b16(256, 1024),
            b16(256, 1024),
            b16(D, HALF),
            b16(HALF, D),
            b16(4, 5, 2, 48, SP),
            b16(4, 5, 2, 48, D),
            sems(4, 13),
            sems(4, 16),
            sems(2),
            sems(2),
        ]
        + [sems(2)] * 11,
        compiler_params=pltpu.CompilerParams(
            collective_id=0, has_side_effects=True, vmem_limit_bytes=56 * 1024 * 1024
        ),
        cost_estimate=pl.CostEstimate(flops=5_000_000_000, bytes_accessed=2_000_000, transcendentals=1_000_000),
    )(tokens, expert_ids.reshape(1, TOK), gate.reshape(1, TOK), ln_gain, w_in[0], w_out[0], image_emb)
    results = (token_grad, gate_grad, in_grad, out_grad)
    token_grad, gate_grad, in_grad, out_grad = pl.pallas_call(
        hand_on,
        out_shape=tuple(jax.ShapeDtypeStruct(r.shape, r.dtype) for r in results),
        in_specs=[vmem] * 4,
        out_specs=(vmem,) * 4,
    )(*results)
    return token_grad, gate_grad.reshape(TOK), in_grad[None], out_grad[None]


def solution(mesh):
    in_specs = (
        P(("dp", "expert"), None),
        P(("dp", "expert"), None),
        P(("dp", "expert")),
        P(),
        P("expert", "dp", None),
        P("expert", "dp", None),
        P(("dp", "expert"), None),
    )
    out_specs = (
        P(("dp", "expert"), None),
        P(("dp", "expert")),
        P("expert", "dp", None),
        P("expert", "dp", None),
    )
    return jax.shard_map(body, mesh=mesh, in_specs=in_specs, out_specs=out_specs, check_vma=False)
```

time: 162 us -> 117 us (0.72)
  Pallas kernels: 155 us -> 117 us
  local copies, waits for them, and re-layouts: 6.04 us -> 0 us
    pallas_call x1, Pallas kernels: 155 us -> 115 us  [body(): pl.pallas_call(kernel, out_shape=(jax.ShapeDtypeStruct((TOK, D), BF16), j...]
    unnamed x15 -> x0, local copies, waits for them, and re-layouts: 5.46 us -> none
    pallas_call x0 -> x1, Pallas kernels: none -> 2.05 us  [body(): pl.pallas_call(hand_on, out_shape=tuple((jax.ShapeDtypeStruct(r.shape, r....]
where the time goes in v2:
time: 117 us
  Pallas kernels  117 us (100%)
    pallas_call x1, Pallas kernels, body(): pl.pallas_call(kernel, out_shape=(jax.ShapeDtypeStruct((TOK, D), BF16), j...  115 us

profile of v2, /device:TPU:1, one launch (start us, length us, event | category | flops | bytes accessed | tf_op | source)
XLA Modules:
  0.0 117.2 jit_solution(13919786511211447775)
XLA Ops:
  0.6 114.5 %shard_map.102 = (bf16[128,768]{1,0:T(8,128)(2,1)}, f32[1,128]{1,0:T(1,128)}, f32[24,3072]{1,0:T(8,128)}, f32[96,768]{1,0:T(8,128)}) custom-call(bf16[128,768]{1,0:T(8,128)(2,1)} %tok.1, s32[1,128]{1,0:T(1,128)} %bitcast.11, f32[1,128]{1,0:T(1,128)} %bitcast.12, f32[768]{0:T(1024)} %gain.1, bf16[24,3072]{1,0:T(8,128)(2,1)} %bitcast.9, ...), custom_call_target="tpu_custom_call" | custom-call | flops 5000000000 | bytes 2000000 | tf_op jit(solution)/shard_map/pallas_call | solution.py:642
  115.2 2.1 %shard_map.103 = (bf16[128,768]{1,0:T(8,128)(2,1)}, f32[1,128]{1,0:T(1,128)}, f32[24,3072]{1,0:T(8,128)}, f32[96,768]{1,0:T(8,128)}) custom-call(bf16[128,768]{1,0:T(8,128)(2,1)} %get-tuple-element.12.refs_0_, f32[1,128]{1,0:T(1,128)} %get-tuple-element.13.refs_1_, f32[24,3072]{1,0:T(8,128)} %get-tuple-element.14.refs_2_, f32[96,768]{1,0:T(8,128)} %get-tuple-element.15.refs_3_), custom_call_target="tpu_custom_call" | custom-call | tf_op jit(solution)/shard_map/pallas_call | solution.py:704

commit v3 on v2

--- a/solution.py
+++ b/solution.py
@@ -23,6 +23,9 @@
 SLOTS = 320
 SP = 384
 EPS = 1e-6
+LINE = (4, 3, 5, 2, 6, 1, 7)
+RING = (8, 9, 7, 6, 10, 5, 11, 4, 12, 3, 13, 2, 14, 1, 15)
+PLANE = (10, 9, 11, 6, 14, 2, 8, 5, 7, 13, 15, 1, 3, 4, 12)
 SCALE = 100.0
 
 
@@ -56,7 +59,7 @@
 
 
 def stack(v):
-    return jnp.concatenate([v[:, :D], v[:, D:]], axis=0).astype(BF16)
+    return jnp.concatenate([v[:, :SP], v[:, SP:]], axis=0).astype(BF16)
 
 
 def unstack(v):
@@ -196,9 +199,9 @@
     sel, vsend, v32, vcame, vback, vfinal, full_in, full_out, imgs, imgb,
     xsend, xr, xs, xt, pre, cdf, act, actt, out32,
     contrib, cjoin, csend, crecv, tall, rsum, rrecv, csum, ccrecv, tb, tbrecv, lb, ob, pb,
-    ib, ibrecv, gi, go, halves, fulls,
+    ib, ibrecv, mixed, mixes, lball, gi, halves, fulls,
     ag_sem, rs_sem, pair_sem, pair2_sem,
-    s_img, s_x, s_c, s_t, s_r, s_cc, s_tb, s_lb, s_ib, s_join, s_share,
+    s_img, s_x, s_c, s_t, s_r, s_cc, s_tb, s_lb, s_ib, s_join, s_share, s_share2, s_m,
 ):
     dp, ex = lax.axis_index("dp"), lax.axis_index("expert")
     xy, h = dp // 2, lax.rem(dp, 2)
@@ -233,8 +236,9 @@
         lax.fori_loop(1, N, step, 0)
 
     class Exchange:
-        def __init__(self, me, dev, src, dst, all_but_one, sem, size=N):
+        def __init__(self, me, dev, src, dst, all_but_one, sem, size=N, order=None):
             self.me, self.dev, self.src, self.dst, self.sem = me, dev, src, dst, sem
+            self.order = order
             self.all_but_one, self.size = all_but_one, size
 
         def copy(self, src, dst, to):
@@ -249,7 +253,11 @@
                 self.copy(self.src(to), self.dst(self.me), to).start()
                 return carry
 
-            lax.fori_loop(1, self.size, step, 0)
+            if self.order is None:
+                lax.fori_loop(1, self.size, step, 0)
+            else:
+                for i in self.order:
+                    step(i, 0)
 
         def wait(self):
             self.copy(self.all_but_one, self.all_but_one, lax.rem(self.me + 1, self.size)).wait_recv()
@@ -279,7 +287,8 @@
         part = win[:, D * g : D * (g + 1)]
         mine.append(dot(part, sel[0]))
         theirs.append(dot(part, sel[1]))
-    vsend[...] = stack(jnp.concatenate(theirs, axis=1))
+    for k in (0, 1):
+        vsend[k] = stack(jnp.concatenate(theirs[2 * k : 2 * k + 2], axis=1))
     for g in range(4):
         v32[pl.ds(pl.multiple_of(24 * h, 8), 24), SP * g : SP * (g + 1)] = mine[g]
     image = img[...].astype(F32)
@@ -338,6 +347,17 @@
 
         return block
 
+    wide = pl.ds(pl.multiple_of(SP * core, TOK), SP)
+
+    def back_at(buf, part):
+        def block(xc, yc, half=None):
+            row = pl.multiple_of((R * yc + xc) * TOK + 64 * part, 32)
+            if half is None:
+                return buf.at[pl.ds(row, 64), wide]
+            return buf.at[pl.ds(pl.multiple_of(row + 32 * half, 32), 32), wide]
+
+        return block
+
     def both(make, buf, at, first, *args):
         other_way = at(buf, 1)
         return (
@@ -350,34 +370,39 @@
     ins = both(Gather, full_in, in_at, 2, full_in.at[pl.ds(0, 96)], fifteen, ag_sem)
 
     other = (2 * xy + 1 - h, ex)
-    pair = pltpu.make_async_remote_copy(
-        src_ref=vsend, dst_ref=vcame, send_sem=pair_sem.at[0], recv_sem=pair_sem.at[1], device_id=other, device_id_type=MESH
-    )
-    pair.start()
+    swaps = [
+        pltpu.make_async_remote_copy(
+            src_ref=vsend.at[k], dst_ref=vcame.at[k], send_sem=pair_sem.at[k], recv_sem=pair_sem.at[2 + k],
+            device_id=other, device_id_type=MESH,
+        )
+        for k in (0, 1)
+    ]
+    for swap in swaps:
+        swap.start()
     for part in outs:
         part.start()
     for part in outs:
         part.second(0)
 
     images = Exchange(j, z_dev, lambda q: rows(imgs, j, 16), lambda s: rows(imgs, s, 16), imgs.at[pl.ds(0, 240)], s_img)
-    images.start()
 
     send_x = Exchange(j, z_dev, lambda q: rows(xsend, lax.rem(q, 8), 16), lambda s: rows(xr, s, 16), xr.at[pl.ds(0, 240)], s_x)
-    send_x.start()
 
     for part in outs:
         part.stage1()
     for part in outs:
         part.stage2()
-    for part in outs:
-        part.stage3(0)
-    pair.wait_recv()
-    v32[pl.ds(pl.multiple_of(24 * (1 - h), 8), 24), :] = unstack(vcame[...])
-    rows(full_in, xy, RI)[...] = v32[...].astype(BF16)
-    for part in ins:
-        part.start()
+    for k in (0, 1):
+        swaps[k].wait_recv()
+        half = slice(D * k, D * (k + 1))
+        v32[pl.ds(pl.multiple_of(24 * (1 - h), 8), 24), half] = unstack(vcame[k])
+        rows(full_in, xy, RI).at[:, half][...] = v32[:, half].astype(BF16)
+        ins[k].start()
+        outs[k].stage3(0)
     for part in ins:
         part.second(0)
+    send_x.start()
+    images.start()
     for i in (1, 2):
         for part in outs:
             part.stage3(i)
@@ -451,10 +476,26 @@
     joined = rows(contrib, core, 128)
     csend[...] = (joined[...].astype(F32) + cjoin[...].astype(F32)).astype(BF16)
     send_c = Exchange(
-        chip, c_dev, lambda q: rows(csend, q, 16), lambda s: rows(crecv, s, 16), crecv.at[pl.ds(0, 112)], s_c, 8
+        chip, c_dev, lambda q: rows(csend, q, 16), lambda s: rows(crecv, s, 16), crecv.at[pl.ds(0, 112)], s_c, 8, LINE
     )
     send_c.start()
     rows(crecv, chip, 16)[...] = rows(csend, chip, 16)[...]
+
+    actt[...] = act[...].T
+    weight1, weight2 = split2(gate_col * pair_of.astype(F32))
+    pad = jnp.zeros((SP - SLOTS, TOK), BF16)
+    weight1 = jnp.concatenate([weight1, pad], axis=0)
+    weight2 = jnp.concatenate([weight2, pad], axis=0)
+
+    def mix(n, carry):
+        part = actt[chunk(n, 256), :]
+        mixed[chunk(n, 256), :] = (dot(part, weight1) + dot(part, weight2)).astype(BF16)
+        return carry
+
+    lax.fori_loop(0, HALF // 256, mix, 0)
+    send_m = Exchange(
+        xy, p_dev, lambda q: rows(mixed, q, RO), lambda s: mixes.at[s], mixes.at[pl.ds(0, N - 1)], s_m
+    )
 
     def slope(n, carry):
         cols = chunk(n, 256)
@@ -462,26 +503,26 @@
         pre[:, cols] = cdf[:, cols] + value * (jnp.exp(-0.5 * value * value) * 0.3989422804014327)
         return carry
 
-    lax.fori_loop(0, HALF // 256, slope, 0)
-
     send_c.wait()
     pooled = (token_sum + jnp.sum(unfold(crecv[...]).reshape(8, PAIR, D), axis=0)) * (1.0 / TEXT)
     q_inv = lax.rsqrt(jnp.sum(pooled * pooled, axis=1, keepdims=True) + EPS)
     unit = pooled * q_inv
     rows(tall, xy, 16)[...] = fold(unit)
-    send_t = Exchange(xy, p_dev, lambda q: rows(tall, xy, 16), lambda s: rows(tall, s, 16), tall.at[pl.ds(0, 240)], s_t)
+    send_t = Exchange(xy, p_dev, lambda q: rows(tall, xy, 16), lambda s: rows(tall, s, 16), tall.at[pl.ds(0, 240)], s_t, N, PLANE)
     send_t.start()
-    actt[...] = act[...].T
+    send_m.start()
+    mixes[pl.ds(xy, 1)] = rows(mixed, xy, RO)[...].reshape(1, RO, TOK)
+    lax.fori_loop(0, 3, slope, 0)
     send_t.wait()
 
     scores = SCALE * dot(unfold(tall[...]).astype(BF16), imgb[...], 1, 1)
     exped = jnp.exp(scores)
     csum[...] = jnp.sum(exped, axis=0, keepdims=True)
     rsum[...] = jnp.sum(exped.T, axis=0, keepdims=True)
-    send_r = Exchange(xy, p_dev, lambda q: rsum, lambda s: rrecv.at[s], rrecv.at[pl.ds(0, N - 1)], s_r)
-    send_cc = Exchange(j, z_dev, lambda q: csum, lambda s: ccrecv.at[s], ccrecv.at[pl.ds(0, N - 1)], s_cc)
+    send_r = Exchange(xy, p_dev, lambda q: rsum, lambda s: rrecv.at[s], rrecv.at[pl.ds(0, N - 1)], s_r, N, PLANE)
+    send_cc = Exchange(j, z_dev, lambda q: csum, lambda s: ccrecv.at[s], ccrecv.at[pl.ds(0, N - 1)], s_cc, N, RING)
+    send_cc.start()
     send_r.start()
-    send_cc.start()
     rrecv[pl.ds(xy, 1)] = rsum[...].reshape(1, 1, TOK)
     ccrecv[pl.ds(j, 1)] = csum[...].reshape(1, 1, TOK)
     text_at = iota((TOK, TOK), 0)
@@ -489,13 +530,14 @@
     diagonal = jnp.where(
         jnp.logical_and(image_at // PAIR == j, text_at == PAIR * xy + lax.rem(image_at, PAIR)), 1.0, 0.0
     )
+    lax.fori_loop(3, 6, slope, 0)
     send_r.wait()
     send_cc.wait()
     row_total = jnp.broadcast_to(jnp.sum(rrecv[...], axis=0), (TOK, TOK)).T
     col_total = jnp.sum(ccrecv[...], axis=0)
     coefs = (0.5 * (exped / row_total + exped / col_total) - diagonal).astype(BF16)
     tb[...] = fold(SCALE * dot(coefs, imgb[...]))
-    send_tb = Exchange(xy, p_dev, lambda q: rows(tb, q, 16), lambda s: rows(tbrecv, s, 16), tbrecv.at[pl.ds(0, 240)], s_tb)
+    send_tb = Exchange(xy, p_dev, lambda q: rows(tb, q, 16), lambda s: rows(tbrecv, s, 16), tbrecv.at[pl.ds(0, 240)], s_tb, N, PLANE)
     send_tb.start()
     rows(tbrecv, xy, 16)[...] = rows(tb, xy, 16)[...]
     send_tb.wait()
@@ -504,7 +546,7 @@
     layer_back = pooled_back * (1.0 / TEXT)
     rows(lb, seat, 16)[...] = fold(layer_back)
     send_lb = Exchange(
-        chip, c_dev, lambda q: rows(lb, seat, 16), lambda s: rows(lb, 8 * core + s, 16), lb.at[pl.ds(0, 112)], s_lb, 8
+        chip, c_dev, lambda q: rows(lb, seat, 16), lambda s: rows(lb, 8 * core + s, 16), lb.at[pl.ds(0, 112)], s_lb, 8, LINE
     )
     send_lb.start()
     send_lb.wait()
@@ -515,14 +557,22 @@
     share.start()
     share.wait_recv()
 
-    slot_back = dot(pair_of, unfold(lb[...]).astype(BF16))
-    ob[0:SLOTS, :] = (gate_col * slot_back).astype(BF16)
-    ob[SLOTS:, :] = jnp.zeros((SP - SLOTS, D), BF16)
+    pairs_back = unfold(lb[...]).astype(BF16)
+    rows(lball, xy, TOK).at[:, wide][...] = jnp.where(core == 0, pairs_back[:, :SP], pairs_back[:, SP:])
+    g_lbs = both(
+        Gather, lball, back_at, 4, lball.at[pl.ds(0, 256), pl.ds(0, SP)], lball.at[pl.ds(0, 960), pl.ds(0, SP)], ag_sem
+    )
+    for part in g_lbs:
+        part.start()
+    for part in g_lbs:
+        part.second(0)
+    slot_back = dot(pair_of, pairs_back)
+    ob[...] = (gate_col * slot_back).astype(BF16)
     pb[SLOTS:, :] = jnp.zeros((SP - SLOTS, HALF), BF16)
 
     def back(n, carry):
         cols = chunk(n, 256)
-        act_back = dot(ob[0:SLOTS, :], full_out[cols, :], 1, 1)
+        act_back = dot(ob[...], full_out[cols, :], 1, 1)
         pb[0:SLOTS, cols] = (act_back * pre[:, cols]).astype(BF16)
         return carry
 
@@ -531,20 +581,11 @@
         gi[:, cols] = dot(xt[...], pb[:, cols]).astype(BF16)
         return carry
 
-    def grad_out(n, carry):
-        go[chunk(n, 256), :] = dot(actt[chunk(n, 256), :], ob[...]).astype(BF16)
-        return carry
-
     s_ins = both(Scatter, gi, in_at, 0, halves, fulls, fifteen, rs_sem)
-    s_outs = both(Scatter, go, out_at, 2, halves, fulls, fifteen, rs_sem)
     for k in (0, 1):
         lax.fori_loop(3 * k, 3 * k + 3, back, 0)
         lax.fori_loop(3 * k, 3 * k + 3, grad_in, 0)
         s_ins[k].start()
-
-    lax.fori_loop(0, HALF // 256, grad_out, 0)
-    for part in s_outs:
-        part.start()
 
     gate_back = jnp.sum(slot_back * out32[...], axis=1, keepdims=True)
     back1 = gate_back.astype(BF16).astype(F32)
@@ -553,36 +594,52 @@
     spread = jnp.zeros((256, 256), F32)
     for m in range(3):
         spread = spread + dot(note_of[m], jnp.where(own_lane, backs[m], 0.0).astype(BF16), 0, 0)
+    for part in g_lbs:
+        part.stage1()
     for p in range(3):
         cols = slice(256 * p, 256 * (p + 1))
         in_back = dot(pb[0:SLOTS, :], full_in[cols, :], 1, 1).astype(BF16)
         ib[:, cols] = in_back[0:256]
         spread = spread + dot(picked[p], in_back[256:SLOTS], 0, 0)
+        if p < 2:
+            for part in s_ins:
+                part.mid(p)
     ib[:, D:] = spread.astype(BF16)
-    send_ib = Exchange(j, z_dev, lambda q: rows(ib, q, 16), lambda s: rows(ibrecv, s, 16), ibrecv.at[pl.ds(0, 240)], s_ib)
+    send_ib = Exchange(
+        j, z_dev, lambda q: rows(ib, q, 16), lambda s: rows(ibrecv, s, 16), ibrecv.at[pl.ds(0, 240)], s_ib
+    )
     send_ib.start()
     rows(ibrecv, j, 16)[...] = rows(ib, j, 16)[...]
-
-    for i in range(4):
+    for part in g_lbs:
+        part.stage2()
+    for i in (2, 3):
         for part in s_ins:
             part.mid(i)
     for i in range(3):
+        for part in g_lbs:
+            part.stage3(i)
         for part in s_ins:
             part.end(i)
-        for part in s_outs:
-            part.mid(i)
-    v32[...] = jnp.concatenate([part.end(3) for part in s_ins], axis=1)
-    vback[...] = stack(v32[pl.ds(pl.multiple_of(24 * (1 - h), 8), 24), :])
-    back_pair = pltpu.make_async_remote_copy(
-        src_ref=vback, dst_ref=vfinal,
-        send_sem=pair2_sem.at[0], recv_sem=pair2_sem.at[1], device_id=other, device_id_type=MESH,
-    )
-    back_pair.start()
-    for part in s_outs:
-        part.mid(3)
-    for i in range(2):
-        for part in s_outs:
-            part.end(i)
+    for part in g_lbs:
+        part.stage3(3)
+    swaps_back = []
+    for k in (0, 1):
+        half = slice(D * k, D * (k + 1))
+        v32[:, half] = s_ins[k].end(3)
+        vback[k] = stack(v32[pl.ds(pl.multiple_of(24 * (1 - h), 8), 24), half])
+        swap = pltpu.make_async_remote_copy(
+            src_ref=vback.at[k], dst_ref=vfinal.at[k], send_sem=pair2_sem.at[k], recv_sem=pair2_sem.at[2 + k],
+            device_id=other, device_id_type=MESH,
+        )
+        swap.start()
+        swaps_back.append(swap)
+    for part in g_lbs:
+        part.stage4()
+    ours = lball.at[:, wide]
+    share2 = pltpu.make_async_remote_copy(
+        src_ref=ours, dst_ref=ours, send_sem=s_share2.at[0], recv_sem=s_share2.at[1], device_id=twin, device_id_type=MESH
+    )
+    share2.start()
 
     send_ib.wait()
     inputs = tok[...].astype(F32)
@@ -605,27 +662,32 @@
     token_gate = jnp.sum(jnp.where(at_slot, gathered, 0.0), axis=1, keepdims=True)
     gg[...] = jnp.broadcast_to(token_gate, (TOK, TOK)).T[0:1]
 
-    for part in s_outs:
-        part.end(2)
-    for k in (0, 1):
-        dwout[48 * k : 48 * (k + 1), :] = s_outs[k].end(3)
+    send_m.wait()
+    factors = jnp.concatenate([mixes[k] for k in range(N)], axis=1)
+    dwout[:, wide] = dot(factors, lball[:, wide])
+    share2.wait_recv()
+    rest = pl.ds(pl.multiple_of(SP * (1 - core), TOK), SP)
+    dwout[:, rest] = dot(factors, lball[:, rest])
     kept = v32[pl.ds(pl.multiple_of(24 * h, 8), 24), :]
     held = []
     for g in range(4):
         hi, lo = split2(kept[:, SP * g : SP * (g + 1)])
         held.append(dot(hi, sel[0], 1, 1) + dot(lo, sel[0], 1, 1))
-    back_pair.wait_recv()
-    came = unstack(vfinal[...])
-    for g in range(4):
-        dwin[:, D * g : D * (g + 1)] = held[g] + dot(came[:, SP * g : SP * (g + 1)].astype(BF16), sel[1], 1, 1)
-
-    pair.wait_send()
+    for k in (0, 1):
+        swaps_back[k].wait_recv()
+        came = unstack(vfinal[k])
+        for g in (0, 1):
+            at = D * (2 * k + g)
+            dwin[:, at : at + D] = held[2 * k + g] + dot(came[:, SP * g : SP * (g + 1)].astype(BF16), sel[1], 1, 1)
+
+    for swap in swaps + swaps_back:
+        swap.wait_send()
     join.wait_send()
     share.wait_send()
-    back_pair.wait_send()
-    for part in outs + ins + s_ins + s_outs:
+    share2.wait_send()
+    for part in outs + ins + g_lbs + s_ins:
         part.sent()
-    for exchange in (images, send_x, send_c, send_t, send_r, send_cc, send_tb, send_lb, send_ib):
+    for exchange in (images, send_x, send_c, send_m, send_t, send_r, send_cc, send_tb, send_lb, send_ib):
         exchange.sent()
 
 
@@ -651,11 +713,11 @@
         out_specs=(vmem,) * 4,
         scratch_shapes=[
             b16(2, D, SP),
-            b16(RI, D),
+            b16(2, 48, SP),
             f32(RI, HALF),
-            b16(RI, D),
-            b16(RI, D),
-            b16(RI, D),
+            b16(2, 48, SP),
+            b16(2, 48, SP),
+            b16(2, 48, SP),
             b16(D, HALF),
             b16(HALF, D),
             b16(256, D // 2),
@@ -681,20 +743,22 @@
             b16(256, D // 2),
             b16(256, D // 2),
             b16(256, D // 2),
-            b16(SP, D),
+            b16(SLOTS, D),
             b16(SP, HALF),
             b16(256, 1024),
             b16(256, 1024),
+            b16(HALF, TOK),
+            b16(N, RO, TOK),
+            b16(N * TOK, D),
             b16(D, HALF),
-            b16(HALF, D),
-            b16(4, 5, 2, 48, SP),
-            b16(4, 5, 2, 48, D),
-            sems(4, 13),
-            sems(4, 16),
-            sems(2),
-            sems(2),
+            b16(2, 5, 2, 48, SP),
+            b16(2, 5, 2, 48, D),
+            sems(6, 13),
+            sems(2, 16),
+            sems(4),
+            sems(4),
         ]
-        + [sems(2)] * 11,
+        + [sems(2)] * 13,
         compiler_params=pltpu.CompilerParams(
             collective_id=0, has_side_effects=True, vmem_limit_bytes=56 * 1024 * 1024
         ),

time: 117 us -> 110 us (0.940)
  Pallas kernels: 117 us -> 110 us
    pallas_call x1, Pallas kernels: 115 us -> 108 us  [body(): pl.pallas_call(kernel, out_shape=(jax.ShapeDtypeStruct((TOK, D), BF16), j...]
where the time goes in v3:
time: 110 us
  Pallas kernels  110 us (100%)
    pallas_call x1, Pallas kernels, body(): pl.pallas_call(kernel, out_shape=(jax.ShapeDtypeStruct((TOK, D), BF16), j...  108 us

profile of v3, /device:TPU:1, one launch (start us, length us, event | category | flops | bytes accessed | tf_op | source)
XLA Modules:
  0.0 110.2 jit_solution(16576719054711452475)
XLA Ops:
  0.6 107.5 %shard_map.102 = (bf16[128,768]{1,0:T(8,128)(2,1)}, f32[1,128]{1,0:T(1,128)}, f32[24,3072]{1,0:T(8,128)}, f32[96,768]{1,0:T(8,128)}) custom-call(bf16[128,768]{1,0:T(8,128)(2,1)} %tok.1, s32[1,128]{1,0:T(1,128)} %bitcast.11, f32[1,128]{1,0:T(1,128)} %bitcast.12, f32[768]{0:T(1024)} %gain.1, bf16[24,3072]{1,0:T(8,128)(2,1)} %bitcast.9, ...), custom_call_target="tpu_custom_call" | custom-call | flops 5000000000 | bytes 2000000 | tf_op jit(solution)/shard_map/pallas_call | solution.py:704
  108.1 2.1 %shard_map.103 = (bf16[128,768]{1,0:T(8,128)(2,1)}, f32[1,128]{1,0:T(1,128)}, f32[24,3072]{1,0:T(8,128)}, f32[96,768]{1,0:T(8,128)}) custom-call(bf16[128,768]{1,0:T(8,128)(2,1)} %get-tuple-element.12.refs_0_, f32[1,128]{1,0:T(1,128)} %get-tuple-element.13.refs_1_, f32[24,3072]{1,0:T(8,128)} %get-tuple-element.14.refs_2_, f32[96,768]{1,0:T(8,128)} %get-tuple-element.15.refs_3_), custom_call_target="tpu_custom_call" | custom-call | tf_op jit(solution)/shard_map/pallas_call | solution.py:768

commit v4 on v3

--- a/solution.py
+++ b/solution.py
@@ -194,8 +194,9 @@
 
 
 def kernel(
-    tok, ids, gate, gain, win, wout, img,
+    tok_in, ids_in, gate_in, gain_in, win_in, wout_in, img_in,
     tg, gg, dwin, dwout,
+    tok, ids, gate, gain, win, wout, img, s_in,
     sel, vsend, v32, vcame, vback, vfinal, full_in, full_out, imgs, imgb,
     xsend, xr, xs, xt, pre, cdf, act, actt, out32,
     contrib, cjoin, csend, crecv, tall, rsum, rrecv, csum, ccrecv, tb, tbrecv, lb, ob, pb,
@@ -228,13 +229,6 @@
     def y_dev(step):
         return p_dev(R * wrap(y + step) + x)
 
-    def each(fn):
-        def step(i, carry):
-            fn(i)
-            return carry
-
-        lax.fori_loop(1, N, step, 0)
-
     class Exchange:
         def __init__(self, me, dev, src, dst, all_but_one, sem, size=N, order=None):
             self.me, self.dev, self.src, self.dst, self.sem = me, dev, src, dst, sem
@@ -270,12 +264,20 @@
 
     barrier = pltpu.get_barrier_semaphore()
 
-    def greet(i):
-        pl.semaphore_signal(barrier, inc=1, device_id=z_dev(lax.rem(j + i, N)), device_id_type=MESH)
-        pl.semaphore_signal(barrier, inc=1, device_id=p_dev(lax.rem(xy + i, N)), device_id_type=MESH)
-
-    each(greet)
-
+    for k in range(N - 1):
+        pl.semaphore_signal(barrier, inc=1, device_id=z_dev(lax.rem(j + RING[k], N)), device_id_type=MESH)
+        pl.semaphore_signal(barrier, inc=1, device_id=p_dev(lax.rem(xy + PLANE[k], N)), device_id_type=MESH)
+
+    loads = [
+        pltpu.make_async_copy(src, dst, s_in.at[k])
+        for k, (src, dst) in enumerate(
+            zip((win_in, tok_in, ids_in, gate_in, gain_in, img_in, wout_in), (win, tok, ids, gate, gain, img, wout))
+        )
+    ]
+    for load in loads:
+        load.start()
+    for load in loads:
+        load.wait()
     rows(full_out, xy, RO)[...] = wout[...]
     source = iota((D, SP), 0)
     column = iota((D, SP), 1)
@@ -510,8 +512,6 @@
     rows(tall, xy, 16)[...] = fold(unit)
     send_t = Exchange(xy, p_dev, lambda q: rows(tall, xy, 16), lambda s: rows(tall, s, 16), tall.at[pl.ds(0, 240)], s_t, N, PLANE)
     send_t.start()
-    send_m.start()
-    mixes[pl.ds(xy, 1)] = rows(mixed, xy, RO)[...].reshape(1, RO, TOK)
     lax.fori_loop(0, 3, slope, 0)
     send_t.wait()
 
@@ -549,6 +549,8 @@
         chip, c_dev, lambda q: rows(lb, seat, 16), lambda s: rows(lb, 8 * core + s, 16), lb.at[pl.ds(0, 112)], s_lb, 8, LINE
     )
     send_lb.start()
+    send_m.start()
+    mixes[pl.ds(xy, 1)] = rows(mixed, xy, RO)[...].reshape(1, RO, TOK)
     send_lb.wait()
     ours = rows(lb, core, 128)
     share = pltpu.make_async_remote_copy(
@@ -576,17 +578,33 @@
         pb[0:SLOTS, cols] = (act_back * pre[:, cols]).astype(BF16)
         return carry
 
-    def grad_in(n, carry):
-        cols = chunk(n, 256)
-        gi[:, cols] = dot(xt[...], pb[:, cols]).astype(BF16)
-        return carry
+    def grad_in(k, step):
+        spots = [(wrap(x + step), b) if k == 0 else (b, wrap(y + step)) for b in range(R)]
+        starts = [pl.multiple_of((R * yc + xc) * RI, 16) for xc, yc in spots]
+        left = jnp.concatenate([xt[pl.ds(at, RI), :] for at in starts], axis=0)
+        value = dot(left, pb[:, D * k : D * (k + 1)]).astype(BF16)
+        for b in range(R):
+            gi[pl.ds(starts[b], RI), D * k : D * (k + 1)] = value[RI * b : RI * (b + 1)]
 
     s_ins = both(Scatter, gi, in_at, 0, halves, fulls, fifteen, rs_sem)
     for k in (0, 1):
         lax.fori_loop(3 * k, 3 * k + 3, back, 0)
-        lax.fori_loop(3 * k, 3 * k + 3, grad_in, 0)
+        grad_in(k, 2)
         s_ins[k].start()
-
+        for step in (1, -1, 0):
+            grad_in(k, step)
+
+    for part in g_lbs:
+        part.stage1()
+    extras = []
+    for p in range(3):
+        cols = slice(256 * p, 256 * (p + 1))
+        in_back = dot(pb[0:SLOTS, :], full_in[cols, :], 1, 1).astype(BF16)
+        ib[:, cols] = in_back[0:256]
+        extras.append(in_back[256:SLOTS])
+        if p < 2:
+            for part in s_ins:
+                part.mid(p)
     gate_back = jnp.sum(slot_back * out32[...], axis=1, keepdims=True)
     back1 = gate_back.astype(BF16).astype(F32)
     back2 = (gate_back - back1).astype(BF16).astype(F32)
@@ -594,16 +612,7 @@
     spread = jnp.zeros((256, 256), F32)
     for m in range(3):
         spread = spread + dot(note_of[m], jnp.where(own_lane, backs[m], 0.0).astype(BF16), 0, 0)
-    for part in g_lbs:
-        part.stage1()
-    for p in range(3):
-        cols = slice(256 * p, 256 * (p + 1))
-        in_back = dot(pb[0:SLOTS, :], full_in[cols, :], 1, 1).astype(BF16)
-        ib[:, cols] = in_back[0:256]
-        spread = spread + dot(picked[p], in_back[256:SLOTS], 0, 0)
-        if p < 2:
-            for part in s_ins:
-                part.mid(p)
+        spread = spread + dot(picked[m], extras[m], 0, 0)
     ib[:, D:] = spread.astype(BF16)
     send_ib = Exchange(
         j, z_dev, lambda q: rows(ib, q, 16), lambda s: rows(ibrecv, s, 16), ibrecv.at[pl.ds(0, 240)], s_ib
@@ -709,9 +718,17 @@
             jax.ShapeDtypeStruct((24, H), F32),
             jax.ShapeDtypeStruct((RO, D), F32),
         ),
-        in_specs=[vmem] * 7,
+        in_specs=[pl.BlockSpec(memory_space=pl.ANY)] * 7,
         out_specs=(vmem,) * 4,
         scratch_shapes=[
+            b16(TOK, D),
+            pltpu.VMEM((1, TOK), jnp.int32),
+            f32(1, TOK),
+            f32(D),
+            b16(24, H),
+            b16(RO, D),
+            b16(PAIR, D),
+            sems(7),
             b16(2, D, SP),
             b16(2, 48, SP),
             f32(RI, HALF),

time: 110 us -> 108 us (0.982)
  Pallas kernels: 110 us -> 108 us
    pallas_call x1, Pallas kernels: 108 us -> 106 us  [body(): pl.pallas_call(kernel, out_shape=(jax.ShapeDtypeStruct((TOK, D), BF16), j...]
where the time goes in v4:
time: 108 us
  Pallas kernels  108 us (100%)
    pallas_call x1, Pallas kernels, body(): pl.pallas_call(kernel, out_shape=(jax.ShapeDtypeStruct((TOK, D), BF16), j...  106 us

profile of v4, /device:TPU:1, one launch (start us, length us, event | category | flops | bytes accessed | tf_op | source)
XLA Modules:
  0.0 108.3 jit_solution(4380260340573946640)
XLA Ops:
  0.6 105.6 %shard_map.102 = (bf16[128,768]{1,0:T(8,128)(2,1)}, f32[1,128]{1,0:T(1,128)}, f32[24,3072]{1,0:T(8,128)}, f32[96,768]{1,0:T(8,128)}) custom-call(bf16[128,768]{1,0:T(8,128)(2,1)} %tok_in.1, s32[1,128]{1,0:T(1,128)} %bitcast.11, f32[1,128]{1,0:T(1,128)} %bitcast.12, f32[768]{0:T(1024)} %gain_in.1, bf16[24,3072]{1,0:T(8,128)(2,1)} %bitcast.9, ...), custom_call_target="tpu_custom_call" | custom-call | flops 5000000000 | bytes 2000000 | tf_op jit(solution)/shard_map/pallas_call | solution.py:713
  106.3 2.1 %shard_map.103 = (bf16[128,768]{1,0:T(8,128)(2,1)}, f32[1,128]{1,0:T(1,128)}, f32[24,3072]{1,0:T(8,128)}, f32[96,768]{1,0:T(8,128)}) custom-call(bf16[128,768]{1,0:T(8,128)(2,1)} %get-tuple-element.12.refs_0_, f32[1,128]{1,0:T(1,128)} %get-tuple-element.13.refs_1_, f32[24,3072]{1,0:T(8,128)} %get-tuple-element.14.refs_2_, f32[96,768]{1,0:T(8,128)} %get-tuple-element.15.refs_3_), custom_call_target="tpu_custom_call" | custom-call | tf_op jit(solution)/shard_map/pallas_call | solution.py:785

commit v5 on v4

--- a/solution.py
+++ b/solution.py
@@ -591,7 +591,8 @@
         lax.fori_loop(3 * k, 3 * k + 3, back, 0)
         grad_in(k, 2)
         s_ins[k].start()
-        for step in (1, -1, 0):
+    for step in (1, -1, 0):
+        for k in (0, 1):
             grad_in(k, step)
 
     for part in g_lbs:

time: 108 us -> 108 us (level)
  no operation moved by 1% of the time
where the time goes in v5:
time: 108 us
  Pallas kernels  107 us (99%)
    pallas_call x1, Pallas kernels, body(): pl.pallas_call(kernel, out_shape=(jax.ShapeDtypeStruct((TOK, D), BF16), j...  105 us

profile of v5, /device:TPU:1, one launch (start us, length us, event | category | flops | bytes accessed | tf_op | source)
XLA Modules:
  0.0 107.6 jit_solution(1726958547712339580)
XLA Ops:
  0.6 105.0 %shard_map.102 = (bf16[128,768]{1,0:T(8,128)(2,1)}, f32[1,128]{1,0:T(1,128)}, f32[24,3072]{1,0:T(8,128)}, f32[96,768]{1,0:T(8,128)}) custom-call(bf16[128,768]{1,0:T(8,128)(2,1)} %tok_in.1, s32[1,128]{1,0:T(1,128)} %bitcast.11, f32[1,128]{1,0:T(1,128)} %bitcast.12, f32[768]{0:T(1024)} %gain_in.1, bf16[24,3072]{1,0:T(8,128)(2,1)} %bitcast.9, ...), custom_call_target="tpu_custom_call" | custom-call | flops 5000000000 | bytes 2000000 | tf_op jit(solution)/shard_map/pallas_call | solution.py:714
  105.6 2.1 %shard_map.103 = (bf16[128,768]{1,0:T(8,128)(2,1)}, f32[1,128]{1,0:T(1,128)}, f32[24,3072]{1,0:T(8,128)}, f32[96,768]{1,0:T(8,128)}) custom-call(bf16[128,768]{1,0:T(8,128)(2,1)} %get-tuple-element.12.refs_0_, f32[1,128]{1,0:T(1,128)} %get-tuple-element.13.refs_1_, f32[24,3072]{1,0:T(8,128)} %get-tuple-element.14.refs_2_, f32[96,768]{1,0:T(8,128)} %get-tuple-element.15.refs_3_), custom_call_target="tpu_custom_call" | custom-call | tf_op jit(solution)/shard_map/pallas_call | solution.py:786

commit v6 on v5

--- a/solution.py
+++ b/solution.py
@@ -484,6 +484,7 @@
     rows(crecv, chip, 16)[...] = rows(csend, chip, 16)[...]
 
     actt[...] = act[...].T
+    pb[SLOTS:, :] = jnp.zeros((SP - SLOTS, HALF), BF16)
     weight1, weight2 = split2(gate_col * pair_of.astype(F32))
     pad = jnp.zeros((SP - SLOTS, TOK), BF16)
     weight1 = jnp.concatenate([weight1, pad], axis=0)
@@ -518,10 +519,10 @@
     scores = SCALE * dot(unfold(tall[...]).astype(BF16), imgb[...], 1, 1)
     exped = jnp.exp(scores)
     csum[...] = jnp.sum(exped, axis=0, keepdims=True)
+    send_cc = Exchange(j, z_dev, lambda q: csum, lambda s: ccrecv.at[s], ccrecv.at[pl.ds(0, N - 1)], s_cc, N, RING)
+    send_cc.start()
     rsum[...] = jnp.sum(exped.T, axis=0, keepdims=True)
     send_r = Exchange(xy, p_dev, lambda q: rsum, lambda s: rrecv.at[s], rrecv.at[pl.ds(0, N - 1)], s_r, N, PLANE)
-    send_cc = Exchange(j, z_dev, lambda q: csum, lambda s: ccrecv.at[s], ccrecv.at[pl.ds(0, N - 1)], s_cc, N, RING)
-    send_cc.start()
     send_r.start()
     rrecv[pl.ds(xy, 1)] = rsum[...].reshape(1, 1, TOK)
     ccrecv[pl.ds(j, 1)] = csum[...].reshape(1, 1, TOK)
@@ -570,7 +571,6 @@
         part.second(0)
     slot_back = dot(pair_of, pairs_back)
     ob[...] = (gate_col * slot_back).astype(BF16)
-    pb[SLOTS:, :] = jnp.zeros((SP - SLOTS, HALF), BF16)
 
     def back(n, carry):
         cols = chunk(n, 256)

time: 108 us -> 108 us (level)
  no operation moved by 1% of the time
where the time goes in v6:
time: 108 us
  Pallas kernels  107 us (99%)
    pallas_call x1, Pallas kernels, body(): pl.pallas_call(kernel, out_shape=(jax.ShapeDtypeStruct((TOK, D), BF16), j...  105 us

profile of v6, /device:TPU:1, one launch (start us, length us, event | category | flops | bytes accessed | tf_op | source)
XLA Modules:
  0.0 107.6 jit_solution(13784207655201338535)
XLA Ops:
  0.6 104.9 %shard_map.102 = (bf16[128,768]{1,0:T(8,128)(2,1)}, f32[1,128]{1,0:T(1,128)}, f32[24,3072]{1,0:T(8,128)}, f32[96,768]{1,0:T(8,128)}) custom-call(bf16[128,768]{1,0:T(8,128)(2,1)} %tok_in.1, s32[1,128]{1,0:T(1,128)} %bitcast.11, f32[1,128]{1,0:T(1,128)} %bitcast.12, f32[768]{0:T(1024)} %gain_in.1, bf16[24,3072]{1,0:T(8,128)(2,1)} %bitcast.9, ...), custom_call_target="tpu_custom_call" | custom-call | flops 5000000000 | bytes 2000000 | tf_op jit(solution)/shard_map/pallas_call | solution.py:714
  105.5 2.1 %shard_map.103 = (bf16[128,768]{1,0:T(8,128)(2,1)}, f32[1,128]{1,0:T(1,128)}, f32[24,3072]{1,0:T(8,128)}, f32[96,768]{1,0:T(8,128)}) custom-call(bf16[128,768]{1,0:T(8,128)(2,1)} %get-tuple-element.12.refs_0_, f32[1,128]{1,0:T(1,128)} %get-tuple-element.13.refs_1_, f32[24,3072]{1,0:T(8,128)} %get-tuple-element.14.refs_2_, f32[96,768]{1,0:T(8,128)} %get-tuple-element.15.refs_3_), custom_call_target="tpu_custom_call" | custom-call | tf_op jit(solution)/shard_map/pallas_call | solution.py:786
